TPU v7x, 32 devices: a whole 2x2x4 slice. The times are simulated.
32 devices in a mesh: pair: 8 (over z, x), tp: 2 (over y), rep: 2 (over core).
Axes of the slice: x: 2, y: 2, z: 4, core: 2. Of those that a mesh axis runs over, the one named last changes fastest.
Arguments:
- normed: bfloat16 [2, 8, 8192], P(None, 'rep', 'pair'), parts along dimension 1, may hold values from -6 to 6
- w_query: bfloat16 [8192, 2048], P('pair', 'tp'), may hold values from -0.0625 to 0.0625
- b_query: float32 [2048], P('tp'), may hold values from -3 to 3
- w_key: bfloat16 [8192, 256], P('pair', 'tp'), may hold values from -0.25 to 0.25
- b_key: float32 [256], P('tp'), may hold values from -8 to 8
- w_value: bfloat16 [8192, 256], P('pair', 'tp'), may hold values from -0.0625 to 0.0625
- b_value: float32 [256], P('tp'), may hold values from -5 to 5
- w_out: bfloat16 [2048, 8192], P('tp', 'pair'), may hold values from -0.5 to 0.5
- pool: bfloat16 [16, 2, 512, 16, 256], P(('rep', 'pair'), 'tp'), parts along dimension 0, as said below
- page_table: int32 [16, 512], P(('rep', 'pair')), parts along dimension 0, may hold values from 0 to 511, as said below
- lengths: int32 [8], P('rep'), parts along dimension 0, may hold values from 8192 to 12286, as said below
- plan: int32 [8, 2], P('rep'), parts along dimension 0, may hold values from 0 to 64, as said below
Outputs:
- attended: float32 [2, 8, 8192], P(None, 'rep', 'pair'), parts along dimension 1
- new_pool: bfloat16 [16, 2, 512, 16, 256], P(('rep', 'pair'), 'tp'), parts along dimension 0
There are 2 independent parts, one for each index of `rep`. A program takes and returns all parts, laid end to end along the dimension named above; an argument that names none is the same for every part. Nothing has to cross between parts.
Inputs may be any that keep to these rules, and one draw needn't show every extreme that they name: `pool`: cached keys (first 128 entries of a slot row, already rotated) and values. `page_table`: each row is an order of the 512 slots of one pool. `lengths`: some request reaches the most. `plan`: some entry reaches the most.
All inputs are finite; a program needn't handle non-finite values.
Results may differ from a plain program's by a relative error of at most 0.011.
The roundings to bfloat16 on the way count: a program that leaves them out, or rounds other values in their place, can miss the bound.
Values may be sent and summed in bfloat16 or wider, within the bound.
No kernel may reach another device: no remote copies, remote signals or barrier semaphores. Data moves between devices by JAX's collectives and lax.ppermute only.
A program may use at most 64 MiB of HBM per device.

v0:
```python
import functools
import math

import jax
import jax.numpy as jnp
from jax import lax
from jax.experimental import pallas as pl
from jax.experimental.pallas import tpu as pltpu
from jax.sharding import PartitionSpec as P

PAGES_HALF = 384
STEPS = 2
SECTION = 64
MOVED_MAX = STEPS * SECTION
FIRST, SECOND, BESIDE, THIRD = 26, 30, 8, 10
NEAR, FAR = 26, 28
BESIDE_AT = FIRST + SECOND
THIRD_AT = BESIDE_AT + BESIDE
NEAR_AT = THIRD_AT + THIRD
FAR_AT = NEAR_AT + NEAR
PIECES = ((FIRST, SECOND), (FAR_AT, FAR))
LATER = ((BESIDE_AT, BESIDE), (THIRD_AT, THIRD), (NEAR_AT, NEAR))
JOINT = 4
CHUNKS = 8
NEG = -1e30

rope_base = 1000000.0

VMEM = pl.BlockSpec(memory_space=pltpu.VMEM)
SMEM = pl.BlockSpec(memory_space=pltpu.SMEM)
HBM = pl.BlockSpec(memory_space=pltpu.HBM)


def in_hbm(*arrays):
    return tuple(pltpu.with_memory_space_constraint(a, pltpu.HBM) for a in arrays)


def params(mib):
    return pltpu.CompilerParams(vmem_limit_bytes=mib * 1024 * 1024)


def moved_pages(plan, request):
    count = plan[0, request]
    for s in range(1, STEPS):
        count = count + plan[s, request]
    return count


def put_pages(table, count, parts, new_pool, sem):
    placed = jnp.int32(0)
    for low, pages in parts:
        here = jnp.clip(count - low, 0, pages.shape[0])

        def start(j, carry):
            slot = table[0, PAGES_HALF + low + j]
            pltpu.make_async_copy(pages.at[j], new_pool.at[slot], sem).start()
            return carry

        lax.fori_loop(0, here, start, 0)
        placed = placed + here

    def wait(j, carry):
        pltpu.make_async_copy(parts[0][1].at[0], new_pool.at[0], sem).wait()
        return carry

    lax.fori_loop(0, placed, wait, 0)


def collect_kernel(table_in, pool, piece, table, sem, page_sem):
    @pl.when(lax.axis_index("pair") >= lax.axis_size("pair") // 2)
    def _():
        table_copy = pltpu.make_async_copy(table_in, table, sem)
        table_copy.start()
        table_copy.wait()

        def start(j, carry):
            pltpu.make_async_copy(pool.at[table[0, j]], piece.at[j], page_sem).start()
            return carry

        lax.fori_loop(0, FIRST, start, 0, unroll=2)
        pltpu.make_async_copy(pool.at[pl.ds(0, FIRST)], piece, page_sem).wait()


def collect(table, pool):
    return pl.pallas_call(
        collect_kernel,
        out_shape=pltpu.VMEM((FIRST,) + pool.shape[1:], pool.dtype),
        in_specs=[HBM] * 2,
        out_specs=VMEM,
        scratch_shapes=[
            pltpu.SMEM(table.shape, table.dtype),
            pltpu.SemaphoreType.DMA,
            pltpu.SemaphoreType.DMA,
        ],
        compiler_params=params(16),
        name="collect",
    )(*in_hbm(table, pool))


def prepare_kernel(w_query, table, plan, normed_in, w_key, w_value, pool, partial, near, far, *refs):
    pieces, (normed, weights, sems, page_sems) = refs[:-4], refs[-4:]
    pairs = partial.shape[0]
    requests = pairs // 2
    head = w_key.shape[1]
    wide = w_query.shape[1]
    loads = [
        pltpu.make_async_copy(normed_in, normed, sems.at[0]),
        pltpu.make_async_copy(w_key, weights.at[:, :head], sems.at[1]),
        pltpu.make_async_copy(w_value, weights.at[:, head:], sems.at[2]),
    ]
    for copy in loads:
        copy.start()

    @pl.when(lax.axis_index("pair") >= requests)
    def _():
        for i, (low, size) in enumerate(PIECES):

            def start(j, carry):
                pltpu.make_async_copy(pool.at[table[0, low + j]], pieces[i].at[j], page_sems.at[i]).start()
                return carry

            lax.fori_loop(0, size, start, 0, unroll=2)

    bits = min(JOINT, requests)
    for code, bound in ((near, NEAR_AT), (far, FAR_AT)):
        total = jnp.int32(0)
        for bit in range(bits):
            most = moved_pages(plan, bit)
            for r in range(bit + bits, requests, bits):
                most = jnp.maximum(most, moved_pages(plan, r))
            total = total + jnp.where(most > bound, 1 << bit, 0)
        code[0] = total
    for copy in loads:
        copy.wait()
    hidden = jnp.concatenate([normed[s].astype(jnp.float32) for s in range(STEPS)], 0).astype(jnp.bfloat16)
    query = jnp.dot(hidden, w_query[...], preferred_element_type=jnp.float32)
    rest = jnp.dot(hidden, weights[...], preferred_element_type=jnp.float32)
    for r in range(requests):
        lines = [slice(s * requests + r, s * requests + r + 1) for s in range(STEPS)]
        query_lines = jnp.concatenate([query[line] for line in lines], 0)
        rest_lines = jnp.concatenate([rest[line] for line in lines], 0)
        for p in range(r, pairs, requests):
            partial[p, :, :wide] = query_lines
            partial[p, :, wide:] = rest_lines

    @pl.when(lax.axis_index("pair") >= requests)
    def _():
        for i, (_, size) in enumerate(PIECES):
            pltpu.make_async_copy(pool.at[pl.ds(0, size)], pieces[i], page_sems.at[i]).wait()


def prepare(table, plan, normed, w_query, w_key, w_value, pool, pairs):
    page = pool.shape[1:]
    wide = w_query.shape[1] + 2 * w_key.shape[1]
    partial, near, far, *pieces = pl.pallas_call(
        prepare_kernel,
        out_shape=(jax.ShapeDtypeStruct((pairs, STEPS, wide), jnp.float32),)
        + (jax.ShapeDtypeStruct((1,), jnp.int32),) * 2
        + tuple(pltpu.VMEM((size,) + page, pool.dtype) for _, size in PIECES),
        in_specs=[VMEM, SMEM, SMEM] + [HBM] * 4,
        out_specs=(VMEM, SMEM, SMEM) + (VMEM,) * len(PIECES),
        scratch_shapes=[
            pltpu.VMEM(normed.shape, normed.dtype),
            pltpu.VMEM((w_key.shape[0], 2 * w_key.shape[1]), w_key.dtype),
            pltpu.SemaphoreType.DMA((3,)),
            pltpu.SemaphoreType.DMA((len(PIECES),)),
        ],
        compiler_params=params(16),
        name="prepare",
    )(w_query, table, plan, *in_hbm(normed, w_key, w_value, pool))
    return partial, near.reshape(()), far.reshape(()), pieces


def page_order(table, slots):
    slot = lax.broadcasted_iota(jnp.int32, (slots, slots), 0)
    holds = jnp.where(slot == table, 1.0, 0.0).astype(jnp.bfloat16)
    index = lax.broadcasted_iota(jnp.int32, (8, slots), 1)
    digit = lax.broadcasted_iota(jnp.int32, (8, slots), 0)
    digits = jnp.where(digit == 0, index // 16, jnp.where(digit == 1, index % 16, 0))
    digits = digits.astype(jnp.float32).astype(jnp.bfloat16)
    return lax.dot_general(digits, holds, (((1,), (1,)), ((), ())), preferred_element_type=jnp.float32)


def attention_kernel(
    lengths, table_in, plan_in, sums, b_query, b_key, b_value, cosine, sine, early, far, pool,
    copies_out, new_pool, fixed, *refs
):
    pieces, refs = refs[: len(LATER)], refs[len(LATER) :]
    held, score, packed, table, slots_of, plan, sems, out_sems, send_sem, page_sem = refs
    slots, page_len, _ = held.shape
    per = slots // CHUNKS
    table_copy = pltpu.make_async_copy(table_in, table, sems.at[CHUNKS])
    table_copy.start()
    slots_copy = pltpu.make_async_copy(table_in, slots_of, sems.at[CHUNKS + 1])
    slots_copy.start()
    plan_copy = pltpu.make_async_copy(plan_in, plan, sems.at[CHUNKS + 2])
    plan_copy.start()
    copies = []
    for c in range(CHUNKS):
        part = pl.ds(c * per, per)
        copies.append(pltpu.make_async_copy(pool.at[part], held.at[part], sems.at[c]))
        copies[-1].start()
    requests = sums.shape[0] // 2
    group, head = b_query.shape
    rows = STEPS * group
    pair_index = lax.axis_index("pair")
    is_source = pair_index >= requests
    request = jnp.where(is_source, pair_index - requests, pair_index)
    half_tokens = PAGES_HALF * page_len
    limit = jnp.where(is_source, lengths[request] - half_tokens, half_tokens)

    blocks = CHUNKS // 2
    block = slots // blocks
    width = block * page_len
    table_copy.wait()
    digits = page_order(table[...], slots)
    digits = jnp.concatenate(
        [digits[d : d + 1, c * block : (c + 1) * block] for d in range(2) for c in range(blocks)], 0
    ).astype(jnp.bfloat16)
    spread = lax.broadcasted_iota(jnp.int32, (block, width), 1) // page_len
    spread = jnp.where(spread == lax.broadcasted_iota(jnp.int32, (block, width), 0), 1.0, 0.0)
    digits = jnp.dot(digits, spread.astype(jnp.bfloat16), preferred_element_type=jnp.float32)
    tokens = (digits[:blocks] * 16.0 + digits[blocks:]).astype(jnp.int32) * page_len
    tokens = tokens + lax.broadcasted_iota(jnp.int32, (blocks, width), 1) % page_len

    total = sums[0]
    for p in range(1, sums.shape[0]):
        total = total + sums[p]
    query = jnp.concatenate(
        [total[s : s + 1, h * head : (h + 1) * head] for s in range(STEPS) for h in range(group)], 0
    )
    query = query + jnp.concatenate([b_query[...]] * STEPS, 0)
    cos_new = cosine[request]
    sin_new = sine[request]
    row = lax.broadcasted_iota(jnp.int32, (rows, head), 0)
    cos_rows = jnp.where(row < group, cos_new[0:1], cos_new[1:2])
    sin_rows = jnp.where(row < group, sin_new[0:1], sin_new[1:2])
    query = (query * cos_rows + pltpu.roll(query, head // 2, 1) * sin_rows).astype(jnp.bfloat16)
    key_new = total[:, group * head : (group + 1) * head] + b_key[...]
    key_new = jnp.concatenate([key_new, jnp.zeros((8 - STEPS, head), jnp.float32)], 0)
    key_new = key_new * cos_new + pltpu.roll(key_new, head // 2, 1) * sin_new
    key_new = key_new.astype(jnp.bfloat16).astype(jnp.float32)
    value_new = total[:, (group + 1) * head :] + b_value[...]
    value_new = value_new.astype(jnp.bfloat16).astype(jnp.float32)
    scale = 1.0 / math.sqrt(head)

    column = lax.broadcasted_iota(jnp.int32, (rows, 1), 0)
    query_wide = query.astype(jnp.float32)
    fresh = []
    for s in range(STEPS):
        dots = jnp.sum(query_wide * key_new[s : s + 1], 1, keepdims=True) * scale
        seen = jnp.logical_and(is_source, column >= s * group)
        fresh.append((jnp.where(seen, dots, NEG), seen))
    row_max = jnp.maximum(fresh[0][0], fresh[1][0])

    stores = []
    for c in range(blocks):
        for i in range(c * CHUNKS // blocks, (c + 1) * CHUNKS // blocks):
            copies[i].wait()
            part = pl.ds(i * per, per)
            stores.append(pltpu.make_async_copy(held.at[part], new_pool.at[part], out_sems.at[i]))
            stores[-1].start()
        keys = held[c * block : (c + 1) * block, :, :head].reshape(width, head)
        part = lax.dot_general(query, keys, (((1,), (1,)), ((), ())), preferred_element_type=jnp.float32)
        part = jnp.where(tokens[c : c + 1] < limit, part * scale, NEG)
        score[:, c * width : (c + 1) * width] = part
        row_max = jnp.maximum(row_max, jnp.max(part, 1, keepdims=True))
    row_sum = jnp.zeros((rows, 1), jnp.float32)
    out = jnp.zeros((rows, head), jnp.float32)
    for s in range(STEPS):
        weight = jnp.where(fresh[s][1], jnp.exp(fresh[s][0] - row_max), 0.0)
        row_sum = row_sum + weight
        out = out + weight.astype(jnp.bfloat16).astype(jnp.float32) * value_new[s : s + 1]
    for c in range(blocks):
        weight = jnp.exp(score[:, c * width : (c + 1) * width] - row_max)
        weight = jnp.where(tokens[c : c + 1] < limit, weight, 0.0)
        row_sum = row_sum + jnp.sum(weight, 1, keepdims=True)
        values = held[c * block : (c + 1) * block, :, head:].reshape(width, head)
        out = out + jnp.dot(weight.astype(jnp.bfloat16), values, preferred_element_type=jnp.float32)

    diagonal = lax.broadcasted_iota(jnp.int32, (rows, head), 1) == row
    for i in range(rows):
        packed[:, i * head : (i + 1) * head] = out[i : i + 1]
    shifted = lax.broadcasted_iota(jnp.int32, (rows, head), 1) == row + rows
    packed[:, rows * head :] = jnp.sum(
        jnp.where(diagonal, row_max, 0.0) + jnp.where(shifted, row_sum, 0.0), 0, keepdims=True
    )
    sends = [
        pltpu.make_async_copy(packed, copies_out.at[p], send_sem.at[p]) for p in range(copies_out.shape[0])
    ]
    for send in sends:
        send.start()

    slots_copy.wait()

    @pl.when(is_source)
    def _():
        for piece, (low, size) in zip(pieces, LATER):

            def take(j, carry):
                piece[j] = held[slots_of[0, low + j]]
                return carry

            lax.fori_loop(0, size, take, 0)
        page_row = lax.broadcasted_iota(jnp.int32, (page_len, 2 * head), 0)
        entries = jnp.concatenate([key_new[:STEPS], value_new], 1)
        offsets = [limit + s for s in range(STEPS)]
        homes = [slots_of[0, offset // page_len] for offset in offsets]
        for i, slot in enumerate((homes[0], homes[-1])):
            page = held[slot].astype(jnp.float32)
            for s, offset in enumerate(offsets):
                here = jnp.logical_and(homes[s] == slot, page_row == offset % page_len)
                page = jnp.where(here, entries[s : s + 1], page)
            fixed[i] = page.astype(held.dtype)

    plan_copy.wait()
    for store in stores:
        store.wait()

    @pl.when(jnp.logical_not(is_source))
    def _():
        put_pages(slots_of, moved_pages(plan, request), [(0, early), (FAR_AT, far)], new_pool, page_sem)

    for send in sends:
        send.wait()


def attend(lengths, table, plan, sums, b_query, b_key, b_value, cosine, sine, early, far, pool):
    group, head = b_query.shape
    rows = STEPS * group
    page = pool.shape[1:]
    return pl.pallas_call(
        attention_kernel,
        out_shape=(
            pltpu.HBM((sums.shape[0], 1, (rows + 1) * head), jnp.float32),
            pltpu.HBM(pool.shape, pool.dtype),
            jax.ShapeDtypeStruct((2,) + page, pool.dtype),
        )
        + tuple(pltpu.VMEM((size,) + page, pool.dtype) for _, size in LATER),
        in_specs=[SMEM, HBM, HBM] + [VMEM] * 8 + [HBM],
        out_specs=(HBM, HBM, VMEM) + (VMEM,) * len(LATER),
        scratch_shapes=[
            pltpu.VMEM(pool.shape, pool.dtype),
            pltpu.VMEM((rows, pool.shape[0] * pool.shape[1]), jnp.float32),
            pltpu.VMEM((1, (rows + 1) * head), jnp.float32),
            pltpu.VMEM(table.shape, table.dtype),
            pltpu.SMEM(table.shape, table.dtype),
            pltpu.SMEM(plan.shape, plan.dtype),
            pltpu.SemaphoreType.DMA((CHUNKS + 3,)),
            pltpu.SemaphoreType.DMA((CHUNKS,)),
            pltpu.SemaphoreType.DMA((sums.shape[0],)),
            pltpu.SemaphoreType.DMA,
        ],
        compiler_params=params(24),
        name="attend",
    )(
        lengths, *in_hbm(table, plan), sums, b_query, b_key, b_value, cosine, sine, early, far, *in_hbm(pool)
    )


def project_kernel(head, parts, w_out, out):
    pairs, _, width = parts.shape
    rows = width // head - 1
    group = rows // STEPS
    requests = pairs // 2
    lane = lax.broadcasted_iota(jnp.int32, (rows, head), 1)
    row = lax.broadcasted_iota(jnp.int32, (rows, head), 0)

    def column(part, shift):
        line = parts[part, :, rows * head :]
        return jnp.sum(jnp.where(lane == row + shift, line, 0.0), 1, keepdims=True)

    lines = [[] for _ in range(STEPS)]
    for r in range(requests):
        tops = [column(part, 0) for part in (r, r + requests)]
        sums = [column(part, rows) for part in (r, r + requests)]
        top = jnp.maximum(*tops)
        weights = [jnp.exp(one - top) for one in tops]
        total = weights[0] * sums[0] + weights[1] * sums[1]
        shares = [weight / total for weight in weights]
        for s in range(STEPS):
            heads = []
            for i in range(s * group, (s + 1) * group):
                here = slice(i * head, (i + 1) * head)
                heads.append(
                    shares[0][i : i + 1] * parts[r, :, here] + shares[1][i : i + 1] * parts[r + requests, :, here]
                )
            lines[s].append(jnp.concatenate(heads, 1))
    attended = jnp.concatenate(sum(lines, []), 0).astype(jnp.bfloat16)
    result = jnp.dot(attended, w_out[...], preferred_element_type=jnp.float32)
    for s in range(STEPS):
        out[s] = result[s * requests : (s + 1) * requests]


def project(parts, w_out, head):
    return pl.pallas_call(
        functools.partial(project_kernel, head),
        out_shape=jax.ShapeDtypeStruct((STEPS, parts.shape[0] // 2, w_out.shape[1]), jnp.float32),
        in_specs=[VMEM, VMEM],
        out_specs=VMEM,
        compiler_params=params(16),
        name="project",
    )(parts, w_out)


def place_kernel(table, plan, lengths, *refs, starts, patch):
    parts, (base, new_pool, sem) = refs[:-3], refs[-3:]
    del base
    pair_index = lax.axis_index("pair")
    requests = lengths.shape[0]

    @pl.when(pair_index < requests)
    def _():
        put_pages(table, moved_pages(plan, pair_index), list(zip(starts, parts)), new_pool, sem)

    if patch:

        @pl.when(pair_index >= requests)
        def _():
            page_len = new_pool.shape[1]
            first = lengths[pair_index - requests] - PAGES_HALF * page_len
            for i, offset in enumerate((first, first + STEPS - 1)):
                slot = table[0, offset // page_len]
                copy = pltpu.make_async_copy(parts[-1].at[i], new_pool.at[slot], sem)
                copy.start()
                copy.wait()


def place(table, plan, lengths, parts, starts, base, fixed=None):
    patch = fixed is not None
    parts = list(parts) + [fixed] * patch
    return pl.pallas_call(
        functools.partial(place_kernel, starts=starts, patch=patch),
        out_shape=pltpu.HBM(base.shape, base.dtype),
        in_specs=[SMEM] * 3 + [VMEM] * len(parts) + [HBM],
        out_specs=HBM,
        scratch_shapes=[
            pltpu.SemaphoreType.DMA,
        ],
        input_output_aliases={3 + len(parts): 0},
        compiler_params=params(16),
        name="place",
    )(table, plan, lengths, *parts, *in_hbm(base))


def blank_kernel(out):
    del out


def blank(like):
    return pl.pallas_call(
        blank_kernel,
        out_shape=jax.ShapeDtypeStruct(like.shape, like.dtype),
        out_specs=pl.BlockSpec(memory_space=pl.ANY),
        name="blank",
    )()


def local(
    normed, w_query, b_query, w_key, b_key, w_value, b_value, w_out, pool, page_table, lengths, plan
):
    pair_count = lax.axis_size("pair")
    tp_count = lax.axis_size("tp")
    requests = pair_count // 2
    head = w_key.shape[1]

    planned = plan.T
    opening = collect(page_table, pool[0, 0])
    partial, near, far, pieces = prepare(
        page_table, planned, normed, w_query, w_key, w_value, pool[0, 0], pair_count
    )
    bits = min(JOINT, requests)

    def tie(*values):
        return lax.optimization_barrier(values)

    def migrate(pages, members=range(requests)):
        return lax.ppermute(pages, "pair", [(r + requests, r) for r in members])

    either = lax.axis_index("rep") == 0

    def gather(values):
        return lax.all_to_all(values, "pair", split_axis=0, concat_axis=0, tiled=True)

    def choose(code, step, *values):
        members = [[r for r in range(requests) if code >> r % bits & 1] for code in range(1 << bits)]
        return lax.switch(code, [functools.partial(step, chosen) for chosen in members], *values)

    def some(members, pages):
        return migrate(pages, members) if members else blank(pages)

    def first_step(members, values, pages):
        return lax.cond(either, gather, gather, values), some(members, pages)

    def second_step(members, values, beside, pages):
        return gather(values), migrate(beside), some(members, pages)

    first = migrate(opening)
    sums, far_pages = choose(far, first_step, partial, pieces[1])
    sums, first = tie(sums, first)
    second = migrate(tie(pieces[0], sums)[0])

    frequency = rope_base ** (-(jnp.arange(head // 2, dtype=jnp.float32) * 2.0 / head))
    steps = jnp.minimum(jnp.arange(8, dtype=jnp.int32), STEPS - 1)
    position = (lengths[:, None] + steps[None, :]).astype(jnp.float32)[..., None]
    angles = position * frequency
    cosine = jnp.cos(angles)
    sine = jnp.sin(angles)
    cosine = jnp.concatenate([cosine, cosine], -1)
    sine = jnp.concatenate([-sine, sine], -1)

    packed, new_pool, fixed, *later = attend(
        lengths,
        page_table,
        planned,
        sums,
        b_query.reshape(-1, head),
        b_key[None, :],
        b_value[None, :],
        cosine,
        sine,
        first,
        far_pages,
        pool[0, 0],
    )
    near, packed = tie(near, packed)
    parts, beside, near_pages = choose(near, second_step, packed, later[0], later[2])
    parts, second = tie(parts, second)
    third = migrate(tie(later[1], parts)[0])
    projected = project(parts, w_out, head)
    here = [second, beside, near_pages]
    starts = [FIRST, BESIDE_AT, NEAR_AT]
    new_pool = place(page_table, planned, lengths, here, starts, new_pool, fixed)
    if tp_count == 2:
        projected = projected + lax.ppermute(projected, "tp", [(0, 1), (1, 0)])
    else:
        projected = lax.psum(projected, "tp")
    third, projected = tie(third, projected)
    new_pool = place(page_table, planned, lengths, [third], [THIRD_AT], new_pool)
    return projected, new_pool[None, None]


def solution(mesh):
    return jax.shard_map(
        local,
        mesh=mesh,
        in_specs=(
            P(None, "rep", "pair"),
            P("pair", "tp"),
            P("tp"),
            P("pair", "tp"),
            P("tp"),
            P("pair", "tp"),
            P("tp"),
            P("tp", "pair"),
            P(("rep", "pair"), "tp", None, None, None),
            P(("rep", "pair"), None),
            P("rep"),
            P("rep", None),
        ),
        out_specs=(P(None, "rep", "pair"), P(("rep", "pair"), "tp", None, None, None)),
        check_vma=False,
    )
```

profile of v0, /device:TPU:0, one launch (start us, length us, event | category | flops | bytes accessed | tf_op | source)
XLA Modules:
  0.0 55.9 jit_solution(8691686777034992825)
XLA Ops:
  0.6 0.0 copy-start.2
  0.6 0.0 copy-start.4
  0.7 0.0 copy-start.1
  0.7 1.4 %collective-permute-start.46 = (bf16[26,16,256]{2,1,0:T(8,128)(2,1)S(1)}, bf16[26,16,256]{2,1,0:T(8,128)(2,1)S(1)}, u32[]{:S(2)}, u32[]{:S(2)}) collective-permute-start(bf16[26,16,256]{2,1,0:T(8,128)(2,1)S(1)} %collect.1), channel_id=1, source_target_pairs={{16,0},{20,4},{24,8},{28,12},{17,1},{21,5},{25,9},{29,13},{18,2},{... | collective-permute-start | bytes 638984 | tf_op jit(solution)/shard_map/ppermute | solution.py:478
  2.2 0.0 copy-done.2
  2.2 0.0 copy-done.4
  2.2 0.1 copy-done.1
  2.3 2.7 %prepare.1 = (f32[8,2,1280]{2,1,0:T(2,128)S(1)}, s32[1]{0:T(128)}, s32[1]{0:T(128)}, bf16[30,16,256]{2,1,0:T(8,128)(2,1)S(1)}, bf16[28,16,256]{2,1,0:T(8,128)(2,1)S(1)}) custom-call(bf16[1024,1024]{1,0:T(8,128)(2,1)S(1)} %copy-done.1, s32[1,512]{1,0:T(1,128)S(1)} %copy-done.2, s32[2,4]{1,0:T(2,128)S(1)} %bitcast.9, bf16[2,4,1024]{2,1,0:T(4,128)(2,1)} %normed_in.1, ...), custom_call_target="tpu_custom_call" | custom-call | tf_op jit(solution)/shard_map/prepare/pallas_call | solution.py:155
  4.9 0.0 copy-start.6
  4.9 0.0 copy-start.7
  4.9 0.0 copy-start.8
  5.0 0.0 copy-start.9
  5.6 17.1 %conditional.18 = (f32[8,2,1280]{2,1,0:T(2,128)}, bf16[28,16,256]{2,1,0:T(8,128)(2,1)}) conditional(s32[]{:T(128)} %bitcast.2, (pred[]{:T(512)}, f32[8,2,1280]{2,1,0:T(2,128)S(1)}) %tuple.238, (pred[]{:T(512)}, f32[8,2,1280]{2,1,0:T(2,128)S(1)}, bf16[28,16,256]{2,1,0:T(8,128)(2,1)S(1)}) %tuple.239, (pred[]{:T(512)}, ...), branch_computations={%region_0.0_spmd, %region_3.0_spmd, %region_6.0_spmd, %region_9.0_... | conditional | flops 1 | bytes 1081413 | solution.py:487
  5.7 1.4 %collective-permute-start.3 = (bf16[28,16,256]{2,1,0:T(8,128)(2,1)S(1)}, bf16[28,16,256]{2,1,0:T(8,128)(2,1)}, u32[]{:S(2)}, u32[]{:S(2)}) collective-permute-start(bf16[28,16,256]{2,1,0:T(8,128)(2,1)S(1)} %get-tuple-element.281), channel_id=1, source_target_pairs={{24,8},{25,9},{26,10},{27,11}} | collective-permute-start | bytes 688136 | tf_op jit(solution)/shard_map/cond/branch_4_fun/ppermute | solution.py:478
  7.0 15.7 %conditional.4 = (f32[8,2,1280]{2,1,0:T(2,128)}) conditional(s32[]{:T(128)} %convert_element_type.42, f32[8,2,1280]{2,1,0:T(2,128)S(1)} %get-tuple-element.280, f32[8,2,1280]{2,1,0:T(2,128)S(1)} %get-tuple-element.280), branch_computations={%region_13.0_spmd, %region_14.0_spmd} | conditional | bytes 163848 | solution.py:493
  7.0 15.7 %all_to_all.201 = f32[8,2,1280]{2,1,0:T(2,128)} all-to-all(f32[8,2,1280]{2,1,0:T(2,128)S(1)} %param.13), channel_id=1, replica_groups=mesh['pair'=8,'tp'=2,'rep'=2] {'pair'}, dimensions={0} | all-to-all | bytes 163840 | tf_op jit(solution)/shard_map/cond/branch_4_fun/cond/branch_1_fun/all_to_all | solution.py:483
  22.8 0.0 collective-permute-done.3
  22.8 0.0 copy-done.6
  22.8 0.0 copy-start
  22.8 0.1 add_convert_fusion
  22.9 0.0 collective-permute-done.46.early
  22.9 1.4 %collective-permute-start.47 = (bf16[30,16,256]{2,1,0:T(8,128)(2,1)S(1)}, bf16[30,16,256]{2,1,0:T(8,128)(2,1)S(1)}, u32[]{:S(2)}, u32[]{:S(2)}) collective-permute-start(bf16[30,16,256]{2,1,0:T(8,128)(2,1)S(1)} %get-tuple-element.406), channel_id=1, source_target_pairs={{16,0},{20,4},{24,8},{28,12},{17,1},{21,5},{25,9},{29,13},{18,2},{... | collective-permute-start | bytes 737288 | tf_op jit(solution)/shard_map/ppermute | solution.py:478
  24.3 0.1 fusion
  24.4 0.1 pad_maximum_fusion
  24.5 0.0 copy-done.7
  24.5 0.0 copy-done.8
  24.5 0.0 copy-done.9
  24.5 0.0 copy-start.3
  24.5 0.0 copy-start.5
  24.6 5.3 %attend.1 = (f32[8,1,2176]{2,1,0:T(1,128)}, bf16[512,16,256]{2,1,0:T(8,128)(2,1)}, bf16[2,16,256]{2,1,0:T(8,128)(2,1)S(1)}, bf16[8,16,256]{2,1,0:T(8,128)(2,1)S(...) custom-call(s32[4]{0:T(128)S(1)} %copy-done.6, s32[1,512]{1,0:T(1,128)} %table.5, s32[2,4]{1,0:T(2,128)} %bitcast.8, ...), custom_call_target="tpu_custom_call" | custom-call | tf_op jit(solution)/shard_map/attend/pallas_call | solution.py:332
  30.5 16.8 %conditional.19 = (f32[8,1,2176]{2,1,0:T(1,128)}, bf16[8,16,256]{2,1,0:T(8,128)(2,1)}, bf16[26,16,256]{2,1,0:T(8,128)(2,1)}) conditional(s32[]{:T(128)} %clamp.11, (f32[8,1,2176]{2,1,0:T(1,128)}, bf16[8,16,256]{2,1,0:T(8,128)(2,1)S(1)}) %tuple.242, (f32[8,1,2176]{2,1,0:T(1,128)}, bf16[8,16,256]{2,1,0:T(8,128)(2,1)S(1)}, ...), branch_computations={%region_48.0_spmd, %region_49.0_spmd, %region_50.0_spmd, %region_5... | conditional | bytes 1323144 | solution.py:487
  30.6 1.3 %collective-permute-start.45 = (bf16[26,16,256]{2,1,0:T(8,128)(2,1)S(1)}, bf16[26,16,256]{2,1,0:T(8,128)(2,1)}, u32[]{:S(2)}, u32[]{:S(2)}) collective-permute-start(bf16[26,16,256]{2,1,0:T(8,128)(2,1)S(1)} %get-tuple-element.361), channel_id=1, source_target_pairs={{16,0},{20,4},{24,8},{28,12},{17,1},{21,5},{25,9},{29,13},{18,2},{... | collective-permute-start | bytes 638984 | tf_op jit(solution)/shard_map/cond/branch_15_fun/ppermute | solution.py:478
  31.9 5.6 %all-to-all-start.47 = ((f32[8,1,2176]{2,1,0:T(1,128)}), f32[8,1,2176]{2,1,0:T(1,128)}, u32[]{:S(2)}, u32[]{:S(2)}) async-start(f32[8,1,2176]{2,1,0:T(1,128)} %get-tuple-element.359), calls=%async_computation.47 | async-start | bytes 139264 | tf_op jit(solution)/shard_map/cond/branch_15_fun/all_to_all | solution.py:483
  37.5 1.3 %collective-permute-start.44 = (bf16[8,16,256]{2,1,0:T(8,128)(2,1)S(1)}, bf16[8,16,256]{2,1,0:T(8,128)(2,1)}, u32[]{:S(2)}, u32[]{:S(2)}) collective-permute-start(bf16[8,16,256]{2,1,0:T(8,128)(2,1)S(1)} %get-tuple-element.360), channel_id=1, source_target_pairs={{16,0},{20,4},{24,8},{28,12},{17,1},{21,5},{25,9},{29,13},{18,2},{... | collective-permute-start | bytes 196616 | tf_op jit(solution)/shard_map/cond/branch_15_fun/ppermute | solution.py:478
  38.8 8.6 %collective-permute-done.44 = bf16[8,16,256]{2,1,0:T(8,128)(2,1)} collective-permute-done((bf16[8,16,256]{2,1,0:T(8,128)(2,1)S(1)}, bf16[8,16,256]{2,1,0:T(8,128)(2,1)}, u32[]{:S(2)}, u32[]{:S(2)}) %collective-permute-start.44) | collective-permute-done | bytes 65568 | tf_op jit(solution)/shard_map/cond/branch_15_fun/ppermute | solution.py:478
  47.4 0.0 all-to-all-done.47
  47.4 0.0 collective-permute-done.45
  47.4 0.0 collective-permute-done.47.refs_0_
  47.4 1.3 %collective-permute-start.48 = (bf16[10,16,256]{2,1,0:T(8,128)(2,1)S(1)}, bf16[10,16,256]{2,1,0:T(8,128)(2,1)S(1)}, u32[]{:S(2)}, u32[]{:S(2)}) collective-permute-start(bf16[10,16,256]{2,1,0:T(8,128)(2,1)S(1)} %get-tuple-element.408), channel_id=1, source_target_pairs={{16,0},{20,4},{24,8},{28,12},{17,1},{21,5},{25,9},{29,13},{18,2},{... | collective-permute-start | bytes 245768 | tf_op jit(solution)/shard_map/ppermute | solution.py:478
  48.7 0.0 copy-done
  48.7 1.4 %project.1 = f32[2,4,1024]{2,1,0:T(4,128)S(1)} custom-call(f32[8,1,2176]{2,1,0:T(1,128)} %get-tuple-element.407.parts, bf16[1024,1024]{1,0:T(8,128)(2,1)S(1)} %copy-done), custom_call_target="tpu_custom_call" | custom-call | tf_op jit(solution)/shard_map/project/pallas_call | solution.py:396
  50.0 1.5 %collective-permute-start.49 = (f32[2,4,1024]{2,1,0:T(4,128)S(1)}, f32[2,4,1024]{2,1,0:T(4,128)S(1)}, u32[]{:S(2)}, u32[]{:S(2)}) collective-permute-start(f32[2,4,1024]{2,1,0:T(4,128)S(1)} %project.1), channel_id=1, source_target_pairs={{0,2},{2,0},{1,3},{3,1},{4,6},{6,4},{5,7},{7,5},{8,10},{10,8},{9,1... | collective-permute-start | bytes 98312 | tf_op jit(solution)/shard_map/ppermute | solution.py:535
  51.6 0.0 copy-done.3
  51.6 0.0 copy-done.5
  51.6 1.9 %place.2.refs_1_ = bf16[512,16,256]{2,1,0:T(8,128)(2,1)} custom-call(s32[1,512]{1,0:T(1,128)S(1)} %copy-done.3, s32[2,4]{1,0:T(2,128)S(1)} %bitcast.10, s32[4]{0:T(128)S(1)} %copy-done.6, bf16[30,16,256]{2,1,0:T(8,128)(2,1)S(1)} %collective-permute-done.47.refs_0_, bf16[8,16,256]{2,1,0:T(8,128)(2,1)} %get-tuple-element.412.refs_1_, ...), custom_call_target="tpu_custom_call", output_to_operand_aliasing={{}: (7, {})} | custom-call | tf_op jit(solution)/shard_map/place/pallas_call | solution.py:432
  53.5 0.5 collective-permute-done.49
  54.0 0.6 %add.23 = f32[2,4,1024]{2,1,0:T(4,128)} add(f32[2,4,1024]{2,1,0:T(4,128)S(1)} %project.1, f32[2,4,1024]{2,1,0:T(4,128)S(1)} %collective-permute-done.49) | non-fusion elementwise | flops 8192 | bytes 98304 | tf_op jit(solution)/shard_map/add | solution.py:535
  54.6 0.0 collective-permute-done.48.refs_0_
  54.6 1.3 %place.3 = bf16[512,16,256]{2,1,0:T(8,128)(2,1)} custom-call(s32[1,512]{1,0:T(1,128)S(1)} %copy-done.3, s32[2,4]{1,0:T(2,128)S(1)} %bitcast.11, s32[4]{0:T(128)S(1)} %copy-done.6, bf16[10,16,256]{2,1,0:T(8,128)(2,1)S(1)} %collective-permute-done.48.refs_0_, bf16[512,16,256]{2,1,0:T(8,128)(2,1)} %place.2.refs_1_), custom_call_target="tpu_custom_call", output_to_operand_aliasing={{}: (4, {})} | custom-call | tf_op jit(solution)/shard_map/place/pallas_call | solution.py:432
  (3 shorter events, 0.0 us)
Async XLA Ops:
  0.6 1.5 %copy-start.2 = (s32[1,512]{1,0:T(1,128)S(1)}, s32[1,512]{1,0:T(1,128)}, u32[]{:S(2)}) copy-start(s32[1,512]{1,0:T(1,128)} %table.5) | copy-start | bytes 6148
  0.6 1.5 %copy-start.4 = (s32[4,2]{0,1:T(2,128)S(1)}, s32[4,2]{0,1:T(2,128)}, u32[]{:S(2)}) copy-start(s32[4,2]{0,1:T(2,128)} %param.87) | copy-start | bytes 100
  0.7 1.6 %copy-start.1 = (bf16[1024,1024]{1,0:T(8,128)(2,1)S(1)}, bf16[1024,1024]{1,0:T(8,128)(2,1)}, u32[]{:S(2)}) copy-start(bf16[1024,1024]{1,0:T(8,128)(2,1)} %w_query.1) | copy-start | bytes 6291460
  0.7 22.2 %collective-permute-start.46 = (bf16[26,16,256]{2,1,0:T(8,128)(2,1)S(1)}, bf16[26,16,256]{2,1,0:T(8,128)(2,1)S(1)}, u32[]{:S(2)}, u32[]{:S(2)}) collective-permute-start(bf16[26,16,256]{2,1,0:T(8,128)(2,1)S(1)} %collect.1), channel_id=1, source_target_pairs={{16,0},{20,4},{24,8},{28,12},{17,1},{21,5},{25,9},{29,13},{18,2},{... | collective-permute-start | bytes 638984 | tf_op jit(solution)/shard_map/ppermute | solution.py:478
  4.9 17.9 %copy-start.6 = (s32[4]{0:T(128)S(1)}, s32[4]{0:T(128)}, u32[]{:S(2)}) copy-start(s32[4]{0:T(128)} %lengths.5) | copy-start | bytes 52
  4.9 19.6 %copy-start.7 = (f32[1024]{0:T(1024)S(1)}, f32[1024]{0:T(1024)}, u32[]{:S(2)}) copy-start(f32[1024]{0:T(1024)} %param.78) | copy-start | bytes 12292
  4.9 19.6 %copy-start.8 = (f32[128]{0:T(128)S(1)}, f32[128]{0:T(128)}, u32[]{:S(2)}) copy-start(f32[128]{0:T(128)} %param.80) | copy-start | bytes 1540
  5.0 19.6 %copy-start.9 = (f32[128]{0:T(128)S(1)}, f32[128]{0:T(128)}, u32[]{:S(2)}) copy-start(f32[128]{0:T(128)} %param.82) | copy-start | bytes 1540
  5.7 17.1 %collective-permute-start.3 = (bf16[28,16,256]{2,1,0:T(8,128)(2,1)S(1)}, bf16[28,16,256]{2,1,0:T(8,128)(2,1)}, u32[]{:S(2)}, u32[]{:S(2)}) collective-permute-start(bf16[28,16,256]{2,1,0:T(8,128)(2,1)S(1)} %get-tuple-element.281), channel_id=1, source_target_pairs={{24,8},{25,9},{26,10},{27,11}} | collective-permute-start | bytes 688136 | tf_op jit(solution)/shard_map/cond/branch_4_fun/ppermute | solution.py:478
  22.8 25.9 %copy-start = (bf16[1024,1024]{1,0:T(8,128)(2,1)S(1)}, bf16[1024,1024]{1,0:T(8,128)(2,1)}, u32[]{:S(2)}) copy-start(bf16[1024,1024]{1,0:T(8,128)(2,1)} %w_out.1) | copy-start | bytes 6291460
  22.9 24.5 %collective-permute-start.47 = (bf16[30,16,256]{2,1,0:T(8,128)(2,1)S(1)}, bf16[30,16,256]{2,1,0:T(8,128)(2,1)S(1)}, u32[]{:S(2)}, u32[]{:S(2)}) collective-permute-start(bf16[30,16,256]{2,1,0:T(8,128)(2,1)S(1)} %get-tuple-element.406), channel_id=1, source_target_pairs={{16,0},{20,4},{24,8},{28,12},{17,1},{21,5},{25,9},{29,13},{18,2},{... | collective-permute-start | bytes 737288 | tf_op jit(solution)/shard_map/ppermute | solution.py:478
  24.5 27.0 %copy-start.3 = (s32[1,512]{1,0:T(1,128)S(1)}, s32[1,512]{1,0:T(1,128)}, u32[]{:S(2)}) copy-start(s32[1,512]{1,0:T(1,128)} %table.5) | copy-start | bytes 6148
  24.5 27.0 %copy-start.5 = (s32[4,2]{0,1:T(2,128)S(1)}, s32[4,2]{0,1:T(2,128)}, u32[]{:S(2)}) copy-start(s32[4,2]{0,1:T(2,128)} %param.87) | copy-start | bytes 100
  30.6 16.8 %collective-permute-start.45 = (bf16[26,16,256]{2,1,0:T(8,128)(2,1)S(1)}, bf16[26,16,256]{2,1,0:T(8,128)(2,1)}, u32[]{:S(2)}, u32[]{:S(2)}) collective-permute-start(bf16[26,16,256]{2,1,0:T(8,128)(2,1)S(1)} %get-tuple-element.361), channel_id=1, source_target_pairs={{16,0},{20,4},{24,8},{28,12},{17,1},{21,5},{25,9},{29,13},{18,2},{... | collective-permute-start | bytes 638984 | tf_op jit(solution)/shard_map/cond/branch_15_fun/ppermute | solution.py:478
  31.9 15.5 %all-to-all-start.47 = ((f32[8,1,2176]{2,1,0:T(1,128)}), f32[8,1,2176]{2,1,0:T(1,128)}, u32[]{:S(2)}, u32[]{:S(2)}) async-start(f32[8,1,2176]{2,1,0:T(1,128)} %get-tuple-element.359), calls=%async_computation.47 | async-start | bytes 139264 | tf_op jit(solution)/shard_map/cond/branch_15_fun/all_to_all | solution.py:483
  37.5 9.9 %collective-permute-start.44 = (bf16[8,16,256]{2,1,0:T(8,128)(2,1)S(1)}, bf16[8,16,256]{2,1,0:T(8,128)(2,1)}, u32[]{:S(2)}, u32[]{:S(2)}) collective-permute-start(bf16[8,16,256]{2,1,0:T(8,128)(2,1)S(1)} %get-tuple-element.360), channel_id=1, source_target_pairs={{16,0},{20,4},{24,8},{28,12},{17,1},{21,5},{25,9},{29,13},{18,2},{... | collective-permute-start | bytes 196616 | tf_op jit(solution)/shard_map/cond/branch_15_fun/ppermute | solution.py:478
  47.4 7.2 %collective-permute-start.48 = (bf16[10,16,256]{2,1,0:T(8,128)(2,1)S(1)}, bf16[10,16,256]{2,1,0:T(8,128)(2,1)S(1)}, u32[]{:S(2)}, u32[]{:S(2)}) collective-permute-start(bf16[10,16,256]{2,1,0:T(8,128)(2,1)S(1)} %get-tuple-element.408), channel_id=1, source_target_pairs={{16,0},{20,4},{24,8},{28,12},{17,1},{21,5},{25,9},{29,13},{18,2},{... | collective-permute-start | bytes 245768 | tf_op jit(solution)/shard_map/ppermute | solution.py:478
  50.0 3.9 %collective-permute-start.49 = (f32[2,4,1024]{2,1,0:T(4,128)S(1)}, f32[2,4,1024]{2,1,0:T(4,128)S(1)}, u32[]{:S(2)}, u32[]{:S(2)}) collective-permute-start(f32[2,4,1024]{2,1,0:T(4,128)S(1)} %project.1), channel_id=1, source_target_pairs={{0,2},{2,0},{1,3},{3,1},{4,6},{6,4},{5,7},{7,5},{8,10},{10,8},{9,1... | collective-permute-start | bytes 98312 | tf_op jit(solution)/shard_map/ppermute | solution.py:535
where the time goes:
time: 55.3 us; the launch traced here: 55.9 us
  blocking collectives  15.7 us (28%)
  starting transfers between devices  15.2 us (27%)
  Pallas kernels  12.6 us (23%)
  waiting for transfers between devices  9.11 us (16%)
  between operations  2.16 us (4%)
  other arithmetic  0.93 us (2%)
    all_to_all x1, blocking collectives, gather(): lax.all_to_all(values, 'pair', split_axis=0, concat_axis=0, tiled=True)  15.7 us
    ppermute x6, waiting for transfers between devices, migrate(): return lax.ppermute(pages, 'pair', [(r + requests, r) for r in members])  8.64 us
    ppermute x6, starting transfers between devices, migrate(): return lax.ppermute(pages, 'pair', [(r + requests, r) for r in members])  8.07 us
    all_to_all x1, starting transfers between devices, gather(): lax.all_to_all(values, 'pair', split_axis=0, concat_axis=0, tiled=True)  5.59 us
    pallas_call x1, Pallas kernels, attend(): pl.pallas_call(attention_kernel, out_shape=(pltpu.HBM((sums.shape[0], 1,...  5.32 us
    pallas_call x2, Pallas kernels, place(): pl.pallas_call(functools.partial(place_kernel, starts=starts, patch=patch...  3.19 us
    pallas_call x1, Pallas kernels, prepare(): pl.pallas_call(prepare_kernel, out_shape=(jax.ShapeDtypeStruct((pairs, ST...  2.66 us
    ppermute x1, starting transfers between devices, local(): projected = projected + lax.ppermute(projected, 'tp', [(0, 1), (1, 0)])  1.53 us
  transfers between devices with their start and end apart: 8, of which 2 were waited for; matrix products, arithmetic and copies ran while one was open for 2% of the time, Pallas kernels for 20%

commit v1 on v0

--- a/solution.py
+++ b/solution.py
@@ -12,7 +12,7 @@
 STEPS = 2
 SECTION = 64
 MOVED_MAX = STEPS * SECTION
-FIRST, SECOND, BESIDE, THIRD = 26, 30, 8, 10
+FIRST, SECOND, BESIDE, THIRD = 26, 32, 9, 7
 NEAR, FAR = 26, 28
 BESIDE_AT = FIRST + SECOND
 THIRD_AT = BESIDE_AT + BESIDE
@@ -97,12 +97,16 @@
     )(*in_hbm(table, pool))
 
 
-def prepare_kernel(w_query, table, plan, normed_in, w_key, w_value, pool, partial, near, far, *refs):
-    pieces, (normed, weights, sems, page_sems) = refs[:-4], refs[-4:]
+def prepare_kernel(w_query, table_in, plan_in, normed_in, w_key, w_value, pool, partial, near, far, *refs):
+    pieces, (table, plan, normed, weights, index_sems, sems, page_sems) = refs[:-7], refs[-7:]
     pairs = partial.shape[0]
     requests = pairs // 2
     head = w_key.shape[1]
     wide = w_query.shape[1]
+    table_copy = pltpu.make_async_copy(table_in, table, index_sems.at[0])
+    plan_copy = pltpu.make_async_copy(plan_in, plan, index_sems.at[1])
+    table_copy.start()
+    plan_copy.start()
     loads = [
         pltpu.make_async_copy(normed_in, normed, sems.at[0]),
         pltpu.make_async_copy(w_key, weights.at[:, :head], sems.at[1]),
@@ -110,6 +114,7 @@
     ]
     for copy in loads:
         copy.start()
+    table_copy.wait()
 
     @pl.when(lax.axis_index("pair") >= requests)
     def _():
@@ -121,6 +126,7 @@
 
             lax.fori_loop(0, size, start, 0, unroll=2)
 
+    plan_copy.wait()
     bits = min(JOINT, requests)
     for code, bound in ((near, NEAR_AT), (far, FAR_AT)):
         total = jnp.int32(0)
@@ -157,17 +163,20 @@
         out_shape=(jax.ShapeDtypeStruct((pairs, STEPS, wide), jnp.float32),)
         + (jax.ShapeDtypeStruct((1,), jnp.int32),) * 2
         + tuple(pltpu.VMEM((size,) + page, pool.dtype) for _, size in PIECES),
-        in_specs=[VMEM, SMEM, SMEM] + [HBM] * 4,
+        in_specs=[VMEM] + [HBM] * 6,
         out_specs=(VMEM, SMEM, SMEM) + (VMEM,) * len(PIECES),
         scratch_shapes=[
+            pltpu.SMEM(table.shape, table.dtype),
+            pltpu.SMEM(plan.shape, plan.dtype),
             pltpu.VMEM(normed.shape, normed.dtype),
             pltpu.VMEM((w_key.shape[0], 2 * w_key.shape[1]), w_key.dtype),
+            pltpu.SemaphoreType.DMA((2,)),
             pltpu.SemaphoreType.DMA((3,)),
             pltpu.SemaphoreType.DMA((len(PIECES),)),
         ],
         compiler_params=params(16),
         name="prepare",
-    )(w_query, table, plan, *in_hbm(normed, w_key, w_value, pool))
+    )(w_query, *in_hbm(table, plan, normed, w_key, w_value, pool))
     return partial, near.reshape(()), far.reshape(()), pieces
 
 

time: 55.3 us -> 55.8 us (level); the launches traced: 55.9 us -> 54.8 us
  waiting for transfers between devices: 9.11 us -> 6.31 us
  blocking collectives: 15.7 us -> 17.9 us
    ppermute x6, waiting for transfers between devices: 8.64 us -> 5.97 us  [migrate(): return lax.ppermute(pages, 'pair', [(r + requests, r) for r in members])]
    all_to_all x1, blocking collectives: 15.7 us -> 17.9 us  [gather(): lax.all_to_all(values, 'pair', split_axis=0, concat_axis=0, tiled=True)]
    pallas_call x1, Pallas kernels: 2.66 us -> 2.1 us  [prepare(): pl.pallas_call(prepare_kernel, out_shape=(jax.ShapeDtypeStruct((pairs, ST...]
where the time goes in v1:
time: 55.8 us; the launch traced here: 54.8 us
  blocking collectives  17.9 us (32%)
  starting transfers between devices  15 us (27%)
  Pallas kernels  12.2 us (22%)
  waiting for transfers between devices  6.31 us (11%)
  between operations  2.13 us (4%)
  other arithmetic  0.93 us (2%)
    all_to_all x1, blocking collectives, gather(): lax.all_to_all(values, 'pair', split_axis=0, concat_axis=0, tiled=True)  17.9 us
    ppermute x6, starting transfers between devices, migrate(): return lax.ppermute(pages, 'pair', [(r + requests, r) for r in members])  7.99 us
    ppermute x6, waiting for transfers between devices, migrate(): return lax.ppermute(pages, 'pair', [(r + requests, r) for r in members])  5.97 us
    all_to_all x1, starting transfers between devices, gather(): lax.all_to_all(values, 'pair', split_axis=0, concat_axis=0, tiled=True)  5.5 us
    pallas_call x1, Pallas kernels, attend(): pl.pallas_call(attention_kernel, out_shape=(pltpu.HBM((sums.shape[0], 1,...  5.45 us
    pallas_call x2, Pallas kernels, place(): pl.pallas_call(functools.partial(place_kernel, starts=starts, patch=patch...  3.29 us
    pallas_call x1, Pallas kernels, prepare(): pl.pallas_call(prepare_kernel, out_shape=(jax.ShapeDtypeStruct((pairs, ST...  2.1 us
    ppermute x1, starting transfers between devices, local(): projected = projected + lax.ppermute(projected, 'tp', [(0, 1), (1, 0)])  1.53 us
  transfers between devices with their start and end apart: 8, of which 2 were waited for; matrix products, arithmetic and copies ran while one was open for 2% of the time, Pallas kernels for 20%

profile of v1, /device:TPU:0, one launch (start us, length us, event | category | flops | bytes accessed | tf_op | source)
XLA Modules:
  0.0 54.8 jit_solution(10756840320008940211)
XLA Ops:
  0.6 0.0 copy-start.1
  0.7 1.4 %collective-permute-start.46 = (bf16[26,16,256]{2,1,0:T(8,128)(2,1)S(1)}, bf16[26,16,256]{2,1,0:T(8,128)(2,1)S(1)}, u32[]{:S(2)}, u32[]{:S(2)}) collective-permute-start(bf16[26,16,256]{2,1,0:T(8,128)(2,1)S(1)} %collect.1), channel_id=1, source_target_pairs={{16,0},{20,4},{24,8},{28,12},{17,1},{21,5},{25,9},{29,13},{18,2},{... | collective-permute-start | bytes 638984 | tf_op jit(solution)/shard_map/ppermute | solution.py:487
  2.1 0.1 copy-done.1
  2.2 2.1 %prepare.1 = (f32[8,2,1280]{2,1,0:T(2,128)S(1)}, s32[1]{0:T(128)}, s32[1]{0:T(128)}, bf16[32,16,256]{2,1,0:T(8,128)(2,1)S(1)}, bf16[28,16,256]{2,1,0:T(8,128)(2,1)S(1)}) custom-call(bf16[1024,1024]{1,0:T(8,128)(2,1)S(1)} %copy-done.1, s32[1,512]{1,0:T(1,128)} %table.3, s32[2,4]{1,0:T(2,128)} %bitcast.8, bf16[2,4,1024]{2,1,0:T(4,128)(2,1)} %normed_in.1, ...), custom_call_target="tpu_custom_call" | custom-call | tf_op jit(solution)/shard_map/prepare/pallas_call | solution.py:161
  4.3 0.0 copy-start.4
  4.3 0.0 copy-start.5
  4.4 0.0 copy-start.6
  4.4 0.0 copy-start.7
  5.0 19.3 %conditional.18 = (f32[8,2,1280]{2,1,0:T(2,128)}, bf16[28,16,256]{2,1,0:T(8,128)(2,1)}) conditional(s32[]{:T(128)} %bitcast.2, (pred[]{:T(512)}, f32[8,2,1280]{2,1,0:T(2,128)S(1)}) %tuple.238, (pred[]{:T(512)}, f32[8,2,1280]{2,1,0:T(2,128)S(1)}, bf16[28,16,256]{2,1,0:T(8,128)(2,1)S(1)}) %tuple.239, (pred[]{:T(512)}, ...), branch_computations={%region_0.0_spmd, %region_3.0_spmd, %region_6.0_spmd, %region_9.0_... | conditional | flops 1 | bytes 1081413 | solution.py:496
  5.1 1.3 %collective-permute-start = (bf16[28,16,256]{2,1,0:T(8,128)(2,1)S(1)}, bf16[28,16,256]{2,1,0:T(8,128)(2,1)}, u32[]{:S(2)}, u32[]{:S(2)}) collective-permute-start(bf16[28,16,256]{2,1,0:T(8,128)(2,1)S(1)} %get-tuple-element.272), channel_id=1, source_target_pairs={{16,0},{17,1},{18,2},{19,3}} | collective-permute-start | bytes 688136 | tf_op jit(solution)/shard_map/cond/branch_1_fun/ppermute | solution.py:487
  6.4 17.9 %conditional.1 = (f32[8,2,1280]{2,1,0:T(2,128)}) conditional(s32[]{:T(128)} %convert_element_type.39, f32[8,2,1280]{2,1,0:T(2,128)S(1)} %get-tuple-element.271, f32[8,2,1280]{2,1,0:T(2,128)S(1)} %get-tuple-element.271), branch_computations={%region_4.0_spmd, %region_5.0_spmd} | conditional | bytes 163848 | solution.py:502
  6.4 17.9 %all_to_all.195 = f32[8,2,1280]{2,1,0:T(2,128)} all-to-all(f32[8,2,1280]{2,1,0:T(2,128)S(1)} %param.4), channel_id=1, replica_groups=mesh['pair'=8,'tp'=2,'rep'=2] {'pair'}, dimensions={0} | all-to-all | bytes 163840 | tf_op jit(solution)/shard_map/cond/branch_1_fun/cond/branch_1_fun/all_to_all | solution.py:492
  24.3 0.0 collective-permute-done
  24.3 0.0 copy-done.4
  24.3 0.0 copy-start
  24.3 0.1 add_convert_fusion
  24.4 0.0 collective-permute-done.46.early
  24.4 1.4 %collective-permute-start.47 = (bf16[32,16,256]{2,1,0:T(8,128)(2,1)S(1)}, bf16[32,16,256]{2,1,0:T(8,128)(2,1)S(1)}, u32[]{:S(2)}, u32[]{:S(2)}) collective-permute-start(bf16[32,16,256]{2,1,0:T(8,128)(2,1)S(1)} %get-tuple-element.406), channel_id=1, source_target_pairs={{16,0},{20,4},{24,8},{28,12},{17,1},{21,5},{25,9},{29,13},{18,2},{... | collective-permute-start | bytes 786440 | tf_op jit(solution)/shard_map/ppermute | solution.py:487
  25.8 0.1 fusion
  26.0 0.1 pad_maximum_fusion
  26.1 0.0 copy-done.5
  26.1 0.0 copy-done.6
  26.1 0.0 copy-done.7
  26.1 0.0 copy-start.2
  26.1 0.0 copy-start.3
  26.1 5.5 %attend.1 = (f32[8,1,2176]{2,1,0:T(1,128)}, bf16[512,16,256]{2,1,0:T(8,128)(2,1)}, bf16[2,16,256]{2,1,0:T(8,128)(2,1)S(1)}, bf16[9,16,256]{2,1,0:T(8,128)(2,1)S(...) custom-call(s32[4]{0:T(128)S(1)} %copy-done.4, s32[1,512]{1,0:T(1,128)} %table.3, s32[2,4]{1,0:T(2,128)} %bitcast.9, ...), custom_call_target="tpu_custom_call" | custom-call | tf_op jit(solution)/shard_map/attend/pallas_call | solution.py:341
  32.2 14.1 %conditional.19 = (f32[8,1,2176]{2,1,0:T(1,128)}, bf16[9,16,256]{2,1,0:T(8,128)(2,1)}, bf16[26,16,256]{2,1,0:T(8,128)(2,1)}) conditional(s32[]{:T(128)} %clamp.11, (f32[8,1,2176]{2,1,0:T(1,128)}, bf16[9,16,256]{2,1,0:T(8,128)(2,1)S(1)}) %tuple.242, (f32[8,1,2176]{2,1,0:T(1,128)}, bf16[9,16,256]{2,1,0:T(8,128)(2,1)S(1)}, ...), branch_computations={%region_48.0_spmd, %region_49.0_spmd, %region_50.0_spmd, %region_5... | conditional | bytes 1355912 | solution.py:496
  32.2 1.3 %collective-permute-start.17 = (bf16[26,16,256]{2,1,0:T(8,128)(2,1)S(1)}, bf16[26,16,256]{2,1,0:T(8,128)(2,1)}, u32[]{:S(2)}, u32[]{:S(2)}) collective-permute-start(bf16[26,16,256]{2,1,0:T(8,128)(2,1)S(1)} %get-tuple-element.319), channel_id=1, source_target_pairs={{16,0},{17,1},{18,2},{19,3}} | collective-permute-start | bytes 638984 | tf_op jit(solution)/shard_map/cond/branch_1_fun/ppermute | solution.py:487
  33.5 5.5 %all-to-all-start.33 = ((f32[8,1,2176]{2,1,0:T(1,128)}), f32[8,1,2176]{2,1,0:T(1,128)}, u32[]{:S(2)}, u32[]{:S(2)}) async-start(f32[8,1,2176]{2,1,0:T(1,128)} %get-tuple-element.317), calls=%async_computation.33 | async-start | bytes 139264 | tf_op jit(solution)/shard_map/cond/branch_1_fun/all_to_all | solution.py:492
  39.0 1.3 %collective-permute-start.16 = (bf16[9,16,256]{2,1,0:T(8,128)(2,1)S(1)}, bf16[9,16,256]{2,1,0:T(8,128)(2,1)}, u32[]{:S(2)}, u32[]{:S(2)}) collective-permute-start(bf16[9,16,256]{2,1,0:T(8,128)(2,1)S(1)} %get-tuple-element.318), channel_id=1, source_target_pairs={{16,0},{20,4},{24,8},{28,12},{17,1},{21,5},{25,9},{29,13},{18,2},{... | collective-permute-start | bytes 221192 | tf_op jit(solution)/shard_map/cond/branch_1_fun/ppermute | solution.py:487
  40.3 6.0 %collective-permute-done.16 = bf16[9,16,256]{2,1,0:T(8,128)(2,1)} collective-permute-done((bf16[9,16,256]{2,1,0:T(8,128)(2,1)S(1)}, bf16[9,16,256]{2,1,0:T(8,128)(2,1)}, u32[]{:S(2)}, u32[]{:S(2)}) %collective-permute-start.16) | collective-permute-done | bytes 73760 | tf_op jit(solution)/shard_map/cond/branch_1_fun/ppermute | solution.py:487
  46.3 0.0 all-to-all-done.33
  46.3 0.0 collective-permute-done.17
  46.3 0.0 collective-permute-done.47.refs_0_
  46.3 1.3 %collective-permute-start.48 = (bf16[7,16,256]{2,1,0:T(8,128)(2,1)S(1)}, bf16[7,16,256]{2,1,0:T(8,128)(2,1)S(1)}, u32[]{:S(2)}, u32[]{:S(2)}) collective-permute-start(bf16[7,16,256]{2,1,0:T(8,128)(2,1)S(1)} %get-tuple-element.408), channel_id=1, source_target_pairs={{16,0},{20,4},{24,8},{28,12},{17,1},{21,5},{25,9},{29,13},{18,2},{... | collective-permute-start | bytes 172040 | tf_op jit(solution)/shard_map/ppermute | solution.py:487
  47.6 0.0 copy-done
  47.6 1.4 %project.1 = f32[2,4,1024]{2,1,0:T(4,128)S(1)} custom-call(f32[8,1,2176]{2,1,0:T(1,128)} %get-tuple-element.407.parts, bf16[1024,1024]{1,0:T(8,128)(2,1)S(1)} %copy-done), custom_call_target="tpu_custom_call" | custom-call | tf_op jit(solution)/shard_map/project/pallas_call | solution.py:405
  49.0 1.5 %collective-permute-start.49 = (f32[2,4,1024]{2,1,0:T(4,128)S(1)}, f32[2,4,1024]{2,1,0:T(4,128)S(1)}, u32[]{:S(2)}, u32[]{:S(2)}) collective-permute-start(f32[2,4,1024]{2,1,0:T(4,128)S(1)} %project.1), channel_id=1, source_target_pairs={{0,2},{2,0},{1,3},{3,1},{4,6},{6,4},{5,7},{7,5},{8,10},{10,8},{9,1... | collective-permute-start | bytes 98312 | tf_op jit(solution)/shard_map/ppermute | solution.py:544
  50.5 0.0 copy-done.2
  50.5 0.0 copy-done.3
  50.5 2.0 %place.2.refs_1_ = bf16[512,16,256]{2,1,0:T(8,128)(2,1)} custom-call(s32[1,512]{1,0:T(1,128)S(1)} %copy-done.2, s32[2,4]{1,0:T(2,128)S(1)} %bitcast.10, s32[4]{0:T(128)S(1)} %copy-done.4, bf16[32,16,256]{2,1,0:T(8,128)(2,1)S(1)} %collective-permute-done.47.refs_0_, bf16[9,16,256]{2,1,0:T(8,128)(2,1)} %get-tuple-element.412.refs_1_, ...), custom_call_target="tpu_custom_call", output_to_operand_aliasing={{}: (7, {})} | custom-call | tf_op jit(solution)/shard_map/place/pallas_call | solution.py:441
  52.5 0.3 collective-permute-done.49
  52.9 0.6 %add.23 = f32[2,4,1024]{2,1,0:T(4,128)} add(f32[2,4,1024]{2,1,0:T(4,128)S(1)} %project.1, f32[2,4,1024]{2,1,0:T(4,128)S(1)} %collective-permute-done.49) | non-fusion elementwise | flops 8192 | bytes 98304 | tf_op jit(solution)/shard_map/add | solution.py:544
  53.5 0.0 collective-permute-done.48.refs_0_
  53.5 1.3 %place.3 = bf16[512,16,256]{2,1,0:T(8,128)(2,1)} custom-call(s32[1,512]{1,0:T(1,128)S(1)} %copy-done.2, s32[2,4]{1,0:T(2,128)S(1)} %bitcast.11, s32[4]{0:T(128)S(1)} %copy-done.4, bf16[7,16,256]{2,1,0:T(8,128)(2,1)S(1)} %collective-permute-done.48.refs_0_, bf16[512,16,256]{2,1,0:T(8,128)(2,1)} %place.2.refs_1_), custom_call_target="tpu_custom_call", output_to_operand_aliasing={{}: (4, {})} | custom-call | tf_op jit(solution)/shard_map/place/pallas_call | solution.py:441
  (3 shorter events, 0.0 us)
Async XLA Ops:
  0.6 1.6 %copy-start.1 = (bf16[1024,1024]{1,0:T(8,128)(2,1)S(1)}, bf16[1024,1024]{1,0:T(8,128)(2,1)}, u32[]{:S(2)}) copy-start(bf16[1024,1024]{1,0:T(8,128)(2,1)} %w_query.1) | copy-start | bytes 6291460
  0.7 23.7 %collective-permute-start.46 = (bf16[26,16,256]{2,1,0:T(8,128)(2,1)S(1)}, bf16[26,16,256]{2,1,0:T(8,128)(2,1)S(1)}, u32[]{:S(2)}, u32[]{:S(2)}) collective-permute-start(bf16[26,16,256]{2,1,0:T(8,128)(2,1)S(1)} %collect.1), channel_id=1, source_target_pairs={{16,0},{20,4},{24,8},{28,12},{17,1},{21,5},{25,9},{29,13},{18,2},{... | collective-permute-start | bytes 638984 | tf_op jit(solution)/shard_map/ppermute | solution.py:487
  4.3 20.0 %copy-start.4 = (s32[4]{0:T(128)S(1)}, s32[4]{0:T(128)}, u32[]{:S(2)}) copy-start(s32[4]{0:T(128)} %lengths.5) | copy-start | bytes 52
  4.3 21.7 %copy-start.5 = (f32[1024]{0:T(1024)S(1)}, f32[1024]{0:T(1024)}, u32[]{:S(2)}) copy-start(f32[1024]{0:T(1024)} %param.78) | copy-start | bytes 12292
  4.4 21.7 %copy-start.6 = (f32[128]{0:T(128)S(1)}, f32[128]{0:T(128)}, u32[]{:S(2)}) copy-start(f32[128]{0:T(128)} %param.80) | copy-start | bytes 1540
  4.4 21.7 %copy-start.7 = (f32[128]{0:T(128)S(1)}, f32[128]{0:T(128)}, u32[]{:S(2)}) copy-start(f32[128]{0:T(128)} %param.82) | copy-start | bytes 1540
  5.1 19.2 %collective-permute-start = (bf16[28,16,256]{2,1,0:T(8,128)(2,1)S(1)}, bf16[28,16,256]{2,1,0:T(8,128)(2,1)}, u32[]{:S(2)}, u32[]{:S(2)}) collective-permute-start(bf16[28,16,256]{2,1,0:T(8,128)(2,1)S(1)} %get-tuple-element.272), channel_id=1, source_target_pairs={{16,0},{17,1},{18,2},{19,3}} | collective-permute-start | bytes 688136 | tf_op jit(solution)/shard_map/cond/branch_1_fun/ppermute | solution.py:487
  24.3 23.3 %copy-start = (bf16[1024,1024]{1,0:T(8,128)(2,1)S(1)}, bf16[1024,1024]{1,0:T(8,128)(2,1)}, u32[]{:S(2)}) copy-start(bf16[1024,1024]{1,0:T(8,128)(2,1)} %w_out.1) | copy-start | bytes 6291460
  24.4 21.9 %collective-permute-start.47 = (bf16[32,16,256]{2,1,0:T(8,128)(2,1)S(1)}, bf16[32,16,256]{2,1,0:T(8,128)(2,1)S(1)}, u32[]{:S(2)}, u32[]{:S(2)}) collective-permute-start(bf16[32,16,256]{2,1,0:T(8,128)(2,1)S(1)} %get-tuple-element.406), channel_id=1, source_target_pairs={{16,0},{20,4},{24,8},{28,12},{17,1},{21,5},{25,9},{29,13},{18,2},{... | collective-permute-start | bytes 786440 | tf_op jit(solution)/shard_map/ppermute | solution.py:487
  26.1 24.4 %copy-start.2 = (s32[1,512]{1,0:T(1,128)S(1)}, s32[1,512]{1,0:T(1,128)}, u32[]{:S(2)}) copy-start(s32[1,512]{1,0:T(1,128)} %table.3) | copy-start | bytes 6148
  26.1 24.4 %copy-start.3 = (s32[4,2]{0,1:T(2,128)S(1)}, s32[4,2]{0,1:T(2,128)}, u32[]{:S(2)}) copy-start(s32[4,2]{0,1:T(2,128)} %param.87) | copy-start | bytes 100
  32.2 14.0 %collective-permute-start.17 = (bf16[26,16,256]{2,1,0:T(8,128)(2,1)S(1)}, bf16[26,16,256]{2,1,0:T(8,128)(2,1)}, u32[]{:S(2)}, u32[]{:S(2)}) collective-permute-start(bf16[26,16,256]{2,1,0:T(8,128)(2,1)S(1)} %get-tuple-element.319), channel_id=1, source_target_pairs={{16,0},{17,1},{18,2},{19,3}} | collective-permute-start | bytes 638984 | tf_op jit(solution)/shard_map/cond/branch_1_fun/ppermute | solution.py:487
  33.5 12.7 %all-to-all-start.33 = ((f32[8,1,2176]{2,1,0:T(1,128)}), f32[8,1,2176]{2,1,0:T(1,128)}, u32[]{:S(2)}, u32[]{:S(2)}) async-start(f32[8,1,2176]{2,1,0:T(1,128)} %get-tuple-element.317), calls=%async_computation.33 | async-start | bytes 139264 | tf_op jit(solution)/shard_map/cond/branch_1_fun/all_to_all | solution.py:492
  39.0 7.2 %collective-permute-start.16 = (bf16[9,16,256]{2,1,0:T(8,128)(2,1)S(1)}, bf16[9,16,256]{2,1,0:T(8,128)(2,1)}, u32[]{:S(2)}, u32[]{:S(2)}) collective-permute-start(bf16[9,16,256]{2,1,0:T(8,128)(2,1)S(1)} %get-tuple-element.318), channel_id=1, source_target_pairs={{16,0},{20,4},{24,8},{28,12},{17,1},{21,5},{25,9},{29,13},{18,2},{... | collective-permute-start | bytes 221192 | tf_op jit(solution)/shard_map/cond/branch_1_fun/ppermute | solution.py:487
  46.3 7.2 %collective-permute-start.48 = (bf16[7,16,256]{2,1,0:T(8,128)(2,1)S(1)}, bf16[7,16,256]{2,1,0:T(8,128)(2,1)S(1)}, u32[]{:S(2)}, u32[]{:S(2)}) collective-permute-start(bf16[7,16,256]{2,1,0:T(8,128)(2,1)S(1)} %get-tuple-element.408), channel_id=1, source_target_pairs={{16,0},{20,4},{24,8},{28,12},{17,1},{21,5},{25,9},{29,13},{18,2},{... | collective-permute-start | bytes 172040 | tf_op jit(solution)/shard_map/ppermute | solution.py:487
  49.0 3.9 %collective-permute-start.49 = (f32[2,4,1024]{2,1,0:T(4,128)S(1)}, f32[2,4,1024]{2,1,0:T(4,128)S(1)}, u32[]{:S(2)}, u32[]{:S(2)}) collective-permute-start(f32[2,4,1024]{2,1,0:T(4,128)S(1)} %project.1), channel_id=1, source_target_pairs={{0,2},{2,0},{1,3},{3,1},{4,6},{6,4},{5,7},{7,5},{8,10},{10,8},{9,1... | collective-permute-start | bytes 98312 | tf_op jit(solution)/shard_map/ppermute | solution.py:544

commit v2 on v1

--- a/solution.py
+++ b/solution.py
@@ -12,14 +12,13 @@
 STEPS = 2
 SECTION = 64
 MOVED_MAX = STEPS * SECTION
-FIRST, SECOND, BESIDE, THIRD = 26, 32, 9, 7
-NEAR, FAR = 26, 28
+FIRST, SECOND, BESIDE = 26, 34, 14
+NEAR, FAR = 25, 29
 BESIDE_AT = FIRST + SECOND
-THIRD_AT = BESIDE_AT + BESIDE
-NEAR_AT = THIRD_AT + THIRD
+NEAR_AT = BESIDE_AT + BESIDE
 FAR_AT = NEAR_AT + NEAR
 PIECES = ((FIRST, SECOND), (FAR_AT, FAR))
-LATER = ((BESIDE_AT, BESIDE), (THIRD_AT, THIRD), (NEAR_AT, NEAR))
+LATER = ((BESIDE_AT, BESIDE), (NEAR_AT, NEAR))
 JOINT = 4
 CHUNKS = 8
 NEG = -1e30
@@ -533,9 +532,8 @@
         pool[0, 0],
     )
     near, packed = tie(near, packed)
-    parts, beside, near_pages = choose(near, second_step, packed, later[0], later[2])
+    parts, beside, near_pages = choose(near, second_step, packed, later[0], later[1])
     parts, second = tie(parts, second)
-    third = migrate(tie(later[1], parts)[0])
     projected = project(parts, w_out, head)
     here = [second, beside, near_pages]
     starts = [FIRST, BESIDE_AT, NEAR_AT]
@@ -544,8 +542,6 @@
         projected = projected + lax.ppermute(projected, "tp", [(0, 1), (1, 0)])
     else:
         projected = lax.psum(projected, "tp")
-    third, projected = tie(third, projected)
-    new_pool = place(page_table, planned, lengths, [third], [THIRD_AT], new_pool)
     return projected, new_pool[None, None]
 
 

time: 55.8 us -> 57.7 us (1.034); the launches traced: 54.8 us -> 58 us
  waiting for transfers between devices: 6.31 us -> 13.6 us
  blocking collectives: 17.9 us -> 16.1 us
  Pallas kernels: 12.2 us -> 10.8 us
  starting transfers between devices: 15 us -> 14.3 us
    ppermute x6 -> x5, waiting for transfers between devices: 5.97 us -> 13.2 us  [migrate(): return lax.ppermute(pages, 'pair', [(r + requests, r) for r in members])]
    all_to_all x1, blocking collectives: 17.9 us -> 16.1 us  [gather(): lax.all_to_all(values, 'pair', split_axis=0, concat_axis=0, tiled=True)]
    pallas_call x2 -> x1, Pallas kernels: 3.29 us -> 1.97 us  [place(): pl.pallas_call(functools.partial(place_kernel, starts=starts, patch=patch...]
    ppermute x6 -> x5, starting transfers between devices: 7.99 us -> 6.77 us  [migrate(): return lax.ppermute(pages, 'pair', [(r + requests, r) for r in members])]
  transfers between devices with their start and end apart: 8 -> 7, of which waited for: 2 -> 2; matrix products, arithmetic and copies ran while one was open for 2% -> 1% of each run, Pallas kernels for 20% -> 16%
where the time goes in v2:
time: 57.7 us; the launch traced here: 58 us
  blocking collectives  16.1 us (28%)
  starting transfers between devices  14.3 us (25%)
  waiting for transfers between devices  13.6 us (24%)
  Pallas kernels  10.8 us (19%)
  between operations  2.12 us (4%)
  other arithmetic  0.93 us (2%)
    all_to_all x1, blocking collectives, gather(): lax.all_to_all(values, 'pair', split_axis=0, concat_axis=0, tiled=True)  16.1 us
    ppermute x5, waiting for transfers between devices, migrate(): return lax.ppermute(pages, 'pair', [(r + requests, r) for r in members])  13.2 us
    ppermute x5, starting transfers between devices, migrate(): return lax.ppermute(pages, 'pair', [(r + requests, r) for r in members])  6.77 us
    all_to_all x1, starting transfers between devices, gather(): lax.all_to_all(values, 'pair', split_axis=0, concat_axis=0, tiled=True)  5.97 us
    pallas_call x1, Pallas kernels, attend(): pl.pallas_call(attention_kernel, out_shape=(pltpu.HBM((sums.shape[0], 1,...  5.32 us
    pallas_call x1, Pallas kernels, prepare(): pl.pallas_call(prepare_kernel, out_shape=(jax.ShapeDtypeStruct((pairs, ST...  2.11 us
    pallas_call x1, Pallas kernels, place(): pl.pallas_call(functools.partial(place_kernel, starts=starts, patch=patch...  1.97 us
    ppermute x1, starting transfers between devices, local(): projected = projected + lax.ppermute(projected, 'tp', [(0, 1), (1, 0)])  1.53 us
  transfers between devices with their start and end apart: 7, of which 2 were waited for; matrix products, arithmetic and copies ran while one was open for 1% of the time, Pallas kernels for 16%

profile of v2, /device:TPU:0, one launch (start us, length us, event | category | flops | bytes accessed | tf_op | source)
XLA Modules:
  0.0 58.0 jit_solution(14656978637958035812)
XLA Ops:
  0.6 0.0 copy-start.1
  0.7 1.4 %collective-permute-start.46 = (bf16[26,16,256]{2,1,0:T(8,128)(2,1)S(1)}, bf16[26,16,256]{2,1,0:T(8,128)(2,1)S(1)}, u32[]{:S(2)}, u32[]{:S(2)}) collective-permute-start(bf16[26,16,256]{2,1,0:T(8,128)(2,1)S(1)} %collect.1), channel_id=1, source_target_pairs={{16,0},{20,4},{24,8},{28,12},{17,1},{21,5},{25,9},{29,13},{18,2},{... | collective-permute-start | bytes 638984 | tf_op jit(solution)/shard_map/ppermute | solution.py:486
  2.1 0.1 copy-done.1
  2.2 2.1 %prepare.1 = (f32[8,2,1280]{2,1,0:T(2,128)S(1)}, s32[1]{0:T(128)}, s32[1]{0:T(128)}, bf16[34,16,256]{2,1,0:T(8,128)(2,1)S(1)}, bf16[29,16,256]{2,1,0:T(8,128)(2,1)S(1)}) custom-call(bf16[1024,1024]{1,0:T(8,128)(2,1)S(1)} %copy-done.1, s32[1,512]{1,0:T(1,128)} %table.1, s32[2,4]{1,0:T(2,128)} %bitcast.8, bf16[2,4,1024]{2,1,0:T(4,128)(2,1)} %normed_in.1, ...), custom_call_target="tpu_custom_call" | custom-call | tf_op jit(solution)/shard_map/prepare/pallas_call | solution.py:160
  4.3 0.0 copy-start.4
  4.4 0.0 copy-start.5
  4.4 0.0 copy-start.6
  4.4 0.0 copy-start.7
  5.1 17.5 %conditional.18 = (f32[8,2,1280]{2,1,0:T(2,128)}, bf16[29,16,256]{2,1,0:T(8,128)(2,1)}) conditional(s32[]{:T(128)} %bitcast.3, (pred[]{:T(512)}, f32[8,2,1280]{2,1,0:T(2,128)S(1)}) %tuple.236, (pred[]{:T(512)}, f32[8,2,1280]{2,1,0:T(2,128)S(1)}, bf16[29,16,256]{2,1,0:T(8,128)(2,1)S(1)}) %tuple.237, (pred[]{:T(512)}, ...), branch_computations={%region_0.0_spmd, %region_3.0_spmd, %region_6.0_spmd, %region_9.0_... | conditional | flops 1 | bytes 1114181 | solution.py:495
  5.1 1.4 %collective-permute-start.1 = (bf16[29,16,256]{2,1,0:T(8,128)(2,1)S(1)}, bf16[29,16,256]{2,1,0:T(8,128)(2,1)}, u32[]{:S(2)}, u32[]{:S(2)}) collective-permute-start(bf16[29,16,256]{2,1,0:T(8,128)(2,1)S(1)} %get-tuple-element.275), channel_id=1, source_target_pairs={{20,4},{21,5},{22,6},{23,7}} | collective-permute-start | bytes 712712 | tf_op jit(solution)/shard_map/cond/branch_2_fun/ppermute | solution.py:486
  6.5 16.1 %conditional.2 = (f32[8,2,1280]{2,1,0:T(2,128)}) conditional(s32[]{:T(128)} %convert_element_type.40, f32[8,2,1280]{2,1,0:T(2,128)S(1)} %get-tuple-element.274, f32[8,2,1280]{2,1,0:T(2,128)S(1)} %get-tuple-element.274), branch_computations={%region_7.0_spmd, %region_8.0_spmd} | conditional | bytes 163848 | solution.py:501
  6.5 16.1 %all_to_all.197 = f32[8,2,1280]{2,1,0:T(2,128)} all-to-all(f32[8,2,1280]{2,1,0:T(2,128)S(1)} %param.7), channel_id=1, replica_groups=mesh['pair'=8,'tp'=2,'rep'=2] {'pair'}, dimensions={0} | all-to-all | bytes 163840 | tf_op jit(solution)/shard_map/cond/branch_2_fun/cond/branch_1_fun/all_to_all | solution.py:491
  22.6 0.0 collective-permute-done.1
  22.6 0.0 copy-done.4
  22.6 0.0 copy-start
  22.6 0.1 add_convert_fusion
  22.7 0.0 collective-permute-done.46.early
  22.7 1.4 %collective-permute-start.47 = (bf16[34,16,256]{2,1,0:T(8,128)(2,1)S(1)}, bf16[34,16,256]{2,1,0:T(8,128)(2,1)S(1)}, u32[]{:S(2)}, u32[]{:S(2)}) collective-permute-start(bf16[34,16,256]{2,1,0:T(8,128)(2,1)S(1)} %get-tuple-element.401), channel_id=1, source_target_pairs={{16,0},{20,4},{24,8},{28,12},{17,1},{21,5},{25,9},{29,13},{18,2},{... | collective-permute-start | bytes 835592 | tf_op jit(solution)/shard_map/ppermute | solution.py:486
  24.1 0.1 fusion
  24.2 0.1 pad_maximum_fusion
  24.3 0.0 copy-done.5
  24.3 0.0 copy-done.6
  24.3 0.0 copy-done.7
  24.3 0.0 copy-start.2
  24.3 0.0 copy-start.3
  24.4 5.3 %attend.1 = (f32[8,1,2176]{2,1,0:T(1,128)}, bf16[512,16,256]{2,1,0:T(8,128)(2,1)}, bf16[2,16,256]{2,1,0:T(8,128)(2,1)S(1)}, bf16[14,16,256]{2,1,0:T(8,128)(2,1)S(1)}, bf16[25,16,256]{2,1,0:T(8,128)(2,1)S(1)}) custom-call(s32[4]{0:T(128)S(1)} %copy-done.4, s32[1,512]{1,0:T(1,128)} %table.1, s32[2,4]{1,0:T(2,128)} %bitcast.9, ...), custom_call_target="tpu_custom_call" | custom-call | tf_op jit(solution)/shard_map/attend/pallas_call | solution.py:340
  30.3 21.8 %conditional.19 = (f32[8,1,2176]{2,1,0:T(1,128)}, bf16[14,16,256]{2,1,0:T(8,128)(2,1)}, bf16[25,16,256]{2,1,0:T(8,128)(2,1)}) conditional(s32[]{:T(128)} %clamp.11, (f32[8,1,2176]{2,1,0:T(1,128)}, bf16[14,16,256]{2,1,0:T(8,128)(2,1)S(1)}) %tuple.240, (f32[8,1,2176]{2,1,0:T(1,128)}, ...), branch_computations={%region_48.0_spmd, %region_49.0_spmd, %region_50.0_spmd, %region_5... | conditional | bytes 1486984 | solution.py:495
  30.4 1.3 %collective-permute-start.29 = (bf16[25,16,256]{2,1,0:T(8,128)(2,1)S(1)}, bf16[25,16,256]{2,1,0:T(8,128)(2,1)}, u32[]{:S(2)}, u32[]{:S(2)}) collective-permute-start(bf16[25,16,256]{2,1,0:T(8,128)(2,1)S(1)} %get-tuple-element.337), channel_id=1, source_target_pairs={{16,0},{20,4},{24,8},{17,1},{21,5},{25,9},{18,2},{22,6},{26,10},{1... | collective-permute-start | bytes 614408 | tf_op jit(solution)/shard_map/cond/branch_7_fun/ppermute | solution.py:486
  31.7 6.0 %all-to-all-start.39 = ((f32[8,1,2176]{2,1,0:T(1,128)}), f32[8,1,2176]{2,1,0:T(1,128)}, u32[]{:S(2)}, u32[]{:S(2)}) async-start(f32[8,1,2176]{2,1,0:T(1,128)} %get-tuple-element.335), calls=%async_computation.39 | async-start | bytes 139264 | tf_op jit(solution)/shard_map/cond/branch_7_fun/all_to_all | solution.py:491
  37.6 1.3 %collective-permute-start.28 = (bf16[14,16,256]{2,1,0:T(8,128)(2,1)S(1)}, bf16[14,16,256]{2,1,0:T(8,128)(2,1)}, u32[]{:S(2)}, u32[]{:S(2)}) collective-permute-start(bf16[14,16,256]{2,1,0:T(8,128)(2,1)S(1)} %get-tuple-element.336), channel_id=1, source_target_pairs={{16,0},{20,4},{24,8},{28,12},{17,1},{21,5},{25,9},{29,13},{18,2},{... | collective-permute-start | bytes 344072 | tf_op jit(solution)/shard_map/cond/branch_7_fun/ppermute | solution.py:486
  38.9 13.2 %collective-permute-done.28 = bf16[14,16,256]{2,1,0:T(8,128)(2,1)} collective-permute-done((bf16[14,16,256]{2,1,0:T(8,128)(2,1)S(1)}, bf16[14,16,256]{2,1,0:T(8,128)(2,1)}, u32[]{:S(2)}, u32[]{:S(2)}) %collective-permute-start.28) | collective-permute-done | bytes 114720 | tf_op jit(solution)/shard_map/cond/branch_7_fun/ppermute | solution.py:486
  52.1 0.0 all-to-all-done.39
  52.1 0.0 collective-permute-done.29
  52.1 0.0 collective-permute-done.47.refs_0_
  52.1 0.0 copy-done
  52.1 1.4 %project.1 = f32[2,4,1024]{2,1,0:T(4,128)S(1)} custom-call(f32[8,1,2176]{2,1,0:T(1,128)} %get-tuple-element.402.parts, bf16[1024,1024]{1,0:T(8,128)(2,1)S(1)} %copy-done), custom_call_target="tpu_custom_call" | custom-call | tf_op jit(solution)/shard_map/project/pallas_call | solution.py:404
  53.5 1.5 %collective-permute-start.48 = (f32[2,4,1024]{2,1,0:T(4,128)S(1)}, f32[2,4,1024]{2,1,0:T(4,128)S(1)}, u32[]{:S(2)}, u32[]{:S(2)}) collective-permute-start(f32[2,4,1024]{2,1,0:T(4,128)S(1)} %project.1), channel_id=1, source_target_pairs={{0,2},{2,0},{1,3},{3,1},{4,6},{6,4},{5,7},{7,5},{8,10},{10,8},{9,1... | collective-permute-start | bytes 98312 | tf_op jit(solution)/shard_map/ppermute | solution.py:542
  55.0 0.0 copy-done.2
  55.0 0.0 copy-done.3
  55.0 2.0 %place.1 = bf16[512,16,256]{2,1,0:T(8,128)(2,1)} custom-call(s32[1,512]{1,0:T(1,128)S(1)} %copy-done.2, s32[2,4]{1,0:T(2,128)S(1)} %bitcast.10, s32[4]{0:T(128)S(1)} %copy-done.4, bf16[34,16,256]{2,1,0:T(8,128)(2,1)S(1)} %collective-permute-done.47.refs_0_, bf16[14,16,256]{2,1,0:T(8,128)(2,1)} %get-tuple-element.404.refs_1_, ...), custom_call_target="tpu_custom_call", output_to_operand_aliasing={{}: (7, {})} | custom-call | tf_op jit(solution)/shard_map/place/pallas_call | solution.py:440
  57.0 0.4 collective-permute-done.48
  57.4 0.6 %add.23 = f32[2,4,1024]{2,1,0:T(4,128)} add(f32[2,4,1024]{2,1,0:T(4,128)S(1)} %project.1, f32[2,4,1024]{2,1,0:T(4,128)S(1)} %collective-permute-done.48) | non-fusion elementwise | flops 8192 | bytes 98304 | tf_op jit(solution)/shard_map/add | solution.py:542
  (3 shorter events, 0.0 us)
Async XLA Ops:
  0.6 1.6 %copy-start.1 = (bf16[1024,1024]{1,0:T(8,128)(2,1)S(1)}, bf16[1024,1024]{1,0:T(8,128)(2,1)}, u32[]{:S(2)}) copy-start(bf16[1024,1024]{1,0:T(8,128)(2,1)} %w_query.1) | copy-start | bytes 6291460
  0.7 22.0 %collective-permute-start.46 = (bf16[26,16,256]{2,1,0:T(8,128)(2,1)S(1)}, bf16[26,16,256]{2,1,0:T(8,128)(2,1)S(1)}, u32[]{:S(2)}, u32[]{:S(2)}) collective-permute-start(bf16[26,16,256]{2,1,0:T(8,128)(2,1)S(1)} %collect.1), channel_id=1, source_target_pairs={{16,0},{20,4},{24,8},{28,12},{17,1},{21,5},{25,9},{29,13},{18,2},{... | collective-permute-start | bytes 638984 | tf_op jit(solution)/shard_map/ppermute | solution.py:486
  4.3 18.2 %copy-start.4 = (s32[4]{0:T(128)S(1)}, s32[4]{0:T(128)}, u32[]{:S(2)}) copy-start(s32[4]{0:T(128)} %lengths.3) | copy-start | bytes 52
  4.4 20.0 %copy-start.5 = (f32[1024]{0:T(1024)S(1)}, f32[1024]{0:T(1024)}, u32[]{:S(2)}) copy-start(f32[1024]{0:T(1024)} %param.78) | copy-start | bytes 12292
  4.4 19.9 %copy-start.6 = (f32[128]{0:T(128)S(1)}, f32[128]{0:T(128)}, u32[]{:S(2)}) copy-start(f32[128]{0:T(128)} %param.80) | copy-start | bytes 1540
  4.4 19.9 %copy-start.7 = (f32[128]{0:T(128)S(1)}, f32[128]{0:T(128)}, u32[]{:S(2)}) copy-start(f32[128]{0:T(128)} %param.82) | copy-start | bytes 1540
  5.1 17.5 %collective-permute-start.1 = (bf16[29,16,256]{2,1,0:T(8,128)(2,1)S(1)}, bf16[29,16,256]{2,1,0:T(8,128)(2,1)}, u32[]{:S(2)}, u32[]{:S(2)}) collective-permute-start(bf16[29,16,256]{2,1,0:T(8,128)(2,1)S(1)} %get-tuple-element.275), channel_id=1, source_target_pairs={{20,4},{21,5},{22,6},{23,7}} | collective-permute-start | bytes 712712 | tf_op jit(solution)/shard_map/cond/branch_2_fun/ppermute | solution.py:486
  22.6 29.6 %copy-start = (bf16[1024,1024]{1,0:T(8,128)(2,1)S(1)}, bf16[1024,1024]{1,0:T(8,128)(2,1)}, u32[]{:S(2)}) copy-start(bf16[1024,1024]{1,0:T(8,128)(2,1)} %w_out.1) | copy-start | bytes 6291460
  22.7 29.5 %collective-permute-start.47 = (bf16[34,16,256]{2,1,0:T(8,128)(2,1)S(1)}, bf16[34,16,256]{2,1,0:T(8,128)(2,1)S(1)}, u32[]{:S(2)}, u32[]{:S(2)}) collective-permute-start(bf16[34,16,256]{2,1,0:T(8,128)(2,1)S(1)} %get-tuple-element.401), channel_id=1, source_target_pairs={{16,0},{20,4},{24,8},{28,12},{17,1},{21,5},{25,9},{29,13},{18,2},{... | collective-permute-start | bytes 835592 | tf_op jit(solution)/shard_map/ppermute | solution.py:486
  24.3 30.7 %copy-start.2 = (s32[1,512]{1,0:T(1,128)S(1)}, s32[1,512]{1,0:T(1,128)}, u32[]{:S(2)}) copy-start(s32[1,512]{1,0:T(1,128)} %table.1) | copy-start | bytes 6148
  24.3 30.7 %copy-start.3 = (s32[4,2]{0,1:T(2,128)S(1)}, s32[4,2]{0,1:T(2,128)}, u32[]{:S(2)}) copy-start(s32[4,2]{0,1:T(2,128)} %param.87) | copy-start | bytes 100
  30.4 21.7 %collective-permute-start.29 = (bf16[25,16,256]{2,1,0:T(8,128)(2,1)S(1)}, bf16[25,16,256]{2,1,0:T(8,128)(2,1)}, u32[]{:S(2)}, u32[]{:S(2)}) collective-permute-start(bf16[25,16,256]{2,1,0:T(8,128)(2,1)S(1)} %get-tuple-element.337), channel_id=1, source_target_pairs={{16,0},{20,4},{24,8},{17,1},{21,5},{25,9},{18,2},{22,6},{26,10},{1... | collective-permute-start | bytes 614408 | tf_op jit(solution)/shard_map/cond/branch_7_fun/ppermute | solution.py:486
  31.7 20.4 %all-to-all-start.39 = ((f32[8,1,2176]{2,1,0:T(1,128)}), f32[8,1,2176]{2,1,0:T(1,128)}, u32[]{:S(2)}, u32[]{:S(2)}) async-start(f32[8,1,2176]{2,1,0:T(1,128)} %get-tuple-element.335), calls=%async_computation.39 | async-start | bytes 139264 | tf_op jit(solution)/shard_map/cond/branch_7_fun/all_to_all | solution.py:491
  37.6 14.5 %collective-permute-start.28 = (bf16[14,16,256]{2,1,0:T(8,128)(2,1)S(1)}, bf16[14,16,256]{2,1,0:T(8,128)(2,1)}, u32[]{:S(2)}, u32[]{:S(2)}) collective-permute-start(bf16[14,16,256]{2,1,0:T(8,128)(2,1)S(1)} %get-tuple-element.336), channel_id=1, source_target_pairs={{16,0},{20,4},{24,8},{28,12},{17,1},{21,5},{25,9},{29,13},{18,2},{... | collective-permute-start | bytes 344072 | tf_op jit(solution)/shard_map/cond/branch_7_fun/ppermute | solution.py:486
  53.5 3.9 %collective-permute-start.48 = (f32[2,4,1024]{2,1,0:T(4,128)S(1)}, f32[2,4,1024]{2,1,0:T(4,128)S(1)}, u32[]{:S(2)}, u32[]{:S(2)}) collective-permute-start(f32[2,4,1024]{2,1,0:T(4,128)S(1)} %project.1), channel_id=1, source_target_pairs={{0,2},{2,0},{1,3},{3,1},{4,6},{6,4},{5,7},{7,5},{8,10},{10,8},{9,1... | collective-permute-start | bytes 98312 | tf_op jit(solution)/shard_map/ppermute | solution.py:542

commit v3 on v1

--- a/solution.py
+++ b/solution.py
@@ -21,7 +21,7 @@
 PIECES = ((FIRST, SECOND), (FAR_AT, FAR))
 LATER = ((BESIDE_AT, BESIDE), (THIRD_AT, THIRD), (NEAR_AT, NEAR))
 JOINT = 4
-CHUNKS = 8
+CHUNKS = 16
 NEG = -1e30
 
 rope_base = 1000000.0

time: 55.8 us -> 54.1 us (0.970)
  blocking collectives: 17.9 us -> 16.1 us
    all_to_all x1, blocking collectives: 17.9 us -> 16.1 us  [gather(): lax.all_to_all(values, 'pair', split_axis=0, concat_axis=0, tiled=True)]
    pallas_call x2, Pallas kernels: 3.29 us -> 2.3 us  [place(): pl.pallas_call(functools.partial(place_kernel, starts=starts, patch=patch...]
  transfers between devices with their start and end apart: 8 -> 8, of which waited for: 2 -> 2; matrix products, arithmetic and copies ran while one was open for 2% -> 2% of each run, Pallas kernels for 20% -> 21%
where the time goes in v3:
time: 54.1 us; the launch traced here: 53.2 us
  blocking collectives  16.1 us (30%)
  starting transfers between devices  15.4 us (28%)
  Pallas kernels  11.8 us (22%)
  waiting for transfers between devices  6.67 us (12%)
  between operations  2.13 us (4%)
  other arithmetic  0.93 us (2%)
    all_to_all x1, blocking collectives, gather(): lax.all_to_all(values, 'pair', split_axis=0, concat_axis=0, tiled=True)  16.1 us
    ppermute x6, starting transfers between devices, migrate(): return lax.ppermute(pages, 'pair', [(r + requests, r) for r in members])  8.12 us
    pallas_call x1, Pallas kernels, attend(): pl.pallas_call(attention_kernel, out_shape=(pltpu.HBM((sums.shape[0], 1,...  5.97 us
    ppermute x6, waiting for transfers between devices, migrate(): return lax.ppermute(pages, 'pair', [(r + requests, r) for r in members])  5.97 us
    all_to_all x1, starting transfers between devices, gather(): lax.all_to_all(values, 'pair', split_axis=0, concat_axis=0, tiled=True)  5.79 us
    pallas_call x2, Pallas kernels, place(): pl.pallas_call(functools.partial(place_kernel, starts=starts, patch=patch...  2.3 us
    pallas_call x1, Pallas kernels, prepare(): pl.pallas_call(prepare_kernel, out_shape=(jax.ShapeDtypeStruct((pairs, ST...  2.1 us
    ppermute x1, starting transfers between devices, local(): projected = projected + lax.ppermute(projected, 'tp', [(0, 1), (1, 0)])  1.53 us
  transfers between devices with their start and end apart: 8, of which 2 were waited for; matrix products, arithmetic and copies ran while one was open for 2% of the time, Pallas kernels for 21%

profile of v3, /device:TPU:0, one launch (start us, length us, event | category | flops | bytes accessed | tf_op | source)
XLA Modules:
  0.0 53.2 jit_solution(15259480316308494076)
XLA Ops:
  0.6 0.0 copy-start.1
  0.7 1.4 %collective-permute-start.46 = (bf16[26,16,256]{2,1,0:T(8,128)(2,1)S(1)}, bf16[26,16,256]{2,1,0:T(8,128)(2,1)S(1)}, u32[]{:S(2)}, u32[]{:S(2)}) collective-permute-start(bf16[26,16,256]{2,1,0:T(8,128)(2,1)S(1)} %collect.1), channel_id=1, source_target_pairs={{16,0},{20,4},{24,8},{28,12},{17,1},{21,5},{25,9},{29,13},{18,2},{... | collective-permute-start | bytes 638984 | tf_op jit(solution)/shard_map/ppermute | solution.py:487
  2.1 0.1 copy-done.1
  2.2 2.1 %prepare.1 = (f32[8,2,1280]{2,1,0:T(2,128)S(1)}, s32[1]{0:T(128)}, s32[1]{0:T(128)}, bf16[32,16,256]{2,1,0:T(8,128)(2,1)S(1)}, bf16[28,16,256]{2,1,0:T(8,128)(2,1)S(1)}) custom-call(bf16[1024,1024]{1,0:T(8,128)(2,1)S(1)} %copy-done.1, s32[1,512]{1,0:T(1,128)} %table.3, s32[2,4]{1,0:T(2,128)} %bitcast.8, bf16[2,4,1024]{2,1,0:T(4,128)(2,1)} %normed_in.1, ...), custom_call_target="tpu_custom_call" | custom-call | tf_op jit(solution)/shard_map/prepare/pallas_call | solution.py:161
  4.3 0.0 copy-start.4
  4.3 0.0 copy-start.5
  4.4 0.0 copy-start.6
  4.4 0.0 copy-start.7
  5.0 17.5 %conditional.18 = (f32[8,2,1280]{2,1,0:T(2,128)}, bf16[28,16,256]{2,1,0:T(8,128)(2,1)}) conditional(s32[]{:T(128)} %bitcast.2, (pred[]{:T(512)}, f32[8,2,1280]{2,1,0:T(2,128)S(1)}) %tuple.238, (pred[]{:T(512)}, f32[8,2,1280]{2,1,0:T(2,128)S(1)}, bf16[28,16,256]{2,1,0:T(8,128)(2,1)S(1)}) %tuple.239, (pred[]{:T(512)}, ...), branch_computations={%region_0.0_spmd, %region_3.0_spmd, %region_6.0_spmd, %region_9.0_... | conditional | flops 1 | bytes 1081413 | solution.py:496
  5.1 1.4 %collective-permute-start.1 = (bf16[28,16,256]{2,1,0:T(8,128)(2,1)S(1)}, bf16[28,16,256]{2,1,0:T(8,128)(2,1)}, u32[]{:S(2)}, u32[]{:S(2)}) collective-permute-start(bf16[28,16,256]{2,1,0:T(8,128)(2,1)S(1)} %get-tuple-element.275), channel_id=1, source_target_pairs={{20,4},{21,5},{22,6},{23,7}} | collective-permute-start | bytes 688136 | tf_op jit(solution)/shard_map/cond/branch_2_fun/ppermute | solution.py:487
  6.4 16.1 %conditional.2 = (f32[8,2,1280]{2,1,0:T(2,128)}) conditional(s32[]{:T(128)} %convert_element_type.40, f32[8,2,1280]{2,1,0:T(2,128)S(1)} %get-tuple-element.274, f32[8,2,1280]{2,1,0:T(2,128)S(1)} %get-tuple-element.274), branch_computations={%region_7.0_spmd, %region_8.0_spmd} | conditional | bytes 163848 | solution.py:502
  6.4 16.1 %all_to_all.197 = f32[8,2,1280]{2,1,0:T(2,128)} all-to-all(f32[8,2,1280]{2,1,0:T(2,128)S(1)} %param.7), channel_id=1, replica_groups=mesh['pair'=8,'tp'=2,'rep'=2] {'pair'}, dimensions={0} | all-to-all | bytes 163840 | tf_op jit(solution)/shard_map/cond/branch_2_fun/cond/branch_1_fun/all_to_all | solution.py:492
  22.6 0.0 collective-permute-done.1
  22.6 0.0 copy-done.4
  22.6 0.0 copy-start
  22.6 0.1 add_convert_fusion
  22.6 0.0 collective-permute-done.46.early
  22.6 1.4 %collective-permute-start.47 = (bf16[32,16,256]{2,1,0:T(8,128)(2,1)S(1)}, bf16[32,16,256]{2,1,0:T(8,128)(2,1)S(1)}, u32[]{:S(2)}, u32[]{:S(2)}) collective-permute-start(bf16[32,16,256]{2,1,0:T(8,128)(2,1)S(1)} %get-tuple-element.406), channel_id=1, source_target_pairs={{16,0},{20,4},{24,8},{28,12},{17,1},{21,5},{25,9},{29,13},{18,2},{... | collective-permute-start | bytes 786440 | tf_op jit(solution)/shard_map/ppermute | solution.py:487
  24.1 0.1 fusion
  24.2 0.1 pad_maximum_fusion
  24.3 0.0 copy-done.5
  24.3 0.0 copy-done.6
  24.3 0.0 copy-done.7
  24.3 0.0 copy-start.2
  24.3 0.0 copy-start.3
  24.3 6.0 %attend.1 = (f32[8,1,2176]{2,1,0:T(1,128)}, bf16[512,16,256]{2,1,0:T(8,128)(2,1)}, bf16[2,16,256]{2,1,0:T(8,128)(2,1)S(1)}, bf16[9,16,256]{2,1,0:T(8,128)(2,1)S(...) custom-call(s32[4]{0:T(128)S(1)} %copy-done.4, s32[1,512]{1,0:T(1,128)} %table.3, s32[2,4]{1,0:T(2,128)} %bitcast.9, ...), custom_call_target="tpu_custom_call" | custom-call | tf_op jit(solution)/shard_map/attend/pallas_call | solution.py:341
  31.0 14.4 %conditional.19 = (f32[8,1,2176]{2,1,0:T(1,128)}, bf16[9,16,256]{2,1,0:T(8,128)(2,1)}, bf16[26,16,256]{2,1,0:T(8,128)(2,1)}) conditional(s32[]{:T(128)} %clamp.11, (f32[8,1,2176]{2,1,0:T(1,128)}, bf16[9,16,256]{2,1,0:T(8,128)(2,1)S(1)}) %tuple.242, (f32[8,1,2176]{2,1,0:T(1,128)}, bf16[9,16,256]{2,1,0:T(8,128)(2,1)S(1)}, ...), branch_computations={%region_48.0_spmd, %region_49.0_spmd, %region_50.0_spmd, %region_5... | conditional | bytes 1355912 | solution.py:496
  31.0 1.4 %collective-permute-start.35 = (bf16[26,16,256]{2,1,0:T(8,128)(2,1)S(1)}, bf16[26,16,256]{2,1,0:T(8,128)(2,1)}, u32[]{:S(2)}, u32[]{:S(2)}) collective-permute-start(bf16[26,16,256]{2,1,0:T(8,128)(2,1)S(1)} %get-tuple-element.346), channel_id=1, source_target_pairs={{20,4},{28,12},{21,5},{29,13},{22,6},{30,14},{23,7},{31,15}} | collective-permute-start | bytes 638984 | tf_op jit(solution)/shard_map/cond/branch_10_fun/ppermute | solution.py:487
  32.4 5.8 %all-to-all-start.42 = ((f32[8,1,2176]{2,1,0:T(1,128)}), f32[8,1,2176]{2,1,0:T(1,128)}, u32[]{:S(2)}, u32[]{:S(2)}) async-start(f32[8,1,2176]{2,1,0:T(1,128)} %get-tuple-element.344), calls=%async_computation.42 | async-start | bytes 139264 | tf_op jit(solution)/shard_map/cond/branch_10_fun/all_to_all | solution.py:492
  38.2 1.3 %collective-permute-start.34 = (bf16[9,16,256]{2,1,0:T(8,128)(2,1)S(1)}, bf16[9,16,256]{2,1,0:T(8,128)(2,1)}, u32[]{:S(2)}, u32[]{:S(2)}) collective-permute-start(bf16[9,16,256]{2,1,0:T(8,128)(2,1)S(1)} %get-tuple-element.345), channel_id=1, source_target_pairs={{16,0},{20,4},{24,8},{28,12},{17,1},{21,5},{25,9},{29,13},{18,2},{... | collective-permute-start | bytes 221192 | tf_op jit(solution)/shard_map/cond/branch_10_fun/ppermute | solution.py:487
  39.4 6.0 %collective-permute-done.34 = bf16[9,16,256]{2,1,0:T(8,128)(2,1)} collective-permute-done((bf16[9,16,256]{2,1,0:T(8,128)(2,1)S(1)}, bf16[9,16,256]{2,1,0:T(8,128)(2,1)}, u32[]{:S(2)}, u32[]{:S(2)}) %collective-permute-start.34) | collective-permute-done | bytes 73760 | tf_op jit(solution)/shard_map/cond/branch_10_fun/ppermute | solution.py:487
  45.4 0.0 all-to-all-done.42
  45.4 0.0 collective-permute-done.35
  45.4 0.0 collective-permute-done.47.refs_0_
  45.4 1.3 %collective-permute-start.48 = (bf16[7,16,256]{2,1,0:T(8,128)(2,1)S(1)}, bf16[7,16,256]{2,1,0:T(8,128)(2,1)S(1)}, u32[]{:S(2)}, u32[]{:S(2)}) collective-permute-start(bf16[7,16,256]{2,1,0:T(8,128)(2,1)S(1)} %get-tuple-element.408), channel_id=1, source_target_pairs={{16,0},{20,4},{24,8},{28,12},{17,1},{21,5},{25,9},{29,13},{18,2},{... | collective-permute-start | bytes 172040 | tf_op jit(solution)/shard_map/ppermute | solution.py:487
  46.7 0.0 copy-done
  46.7 1.4 %project.1 = f32[2,4,1024]{2,1,0:T(4,128)S(1)} custom-call(f32[8,1,2176]{2,1,0:T(1,128)} %get-tuple-element.407.parts, bf16[1024,1024]{1,0:T(8,128)(2,1)S(1)} %copy-done), custom_call_target="tpu_custom_call" | custom-call | tf_op jit(solution)/shard_map/project/pallas_call | solution.py:405
  48.1 1.5 %collective-permute-start.49 = (f32[2,4,1024]{2,1,0:T(4,128)S(1)}, f32[2,4,1024]{2,1,0:T(4,128)S(1)}, u32[]{:S(2)}, u32[]{:S(2)}) collective-permute-start(f32[2,4,1024]{2,1,0:T(4,128)S(1)} %project.1), channel_id=1, source_target_pairs={{0,2},{2,0},{1,3},{3,1},{4,6},{6,4},{5,7},{7,5},{8,10},{10,8},{9,1... | collective-permute-start | bytes 98312 | tf_op jit(solution)/shard_map/ppermute | solution.py:544
  49.6 0.0 copy-done.2
  49.6 0.0 copy-done.3
  49.6 1.7 %place.2.refs_1_ = bf16[512,16,256]{2,1,0:T(8,128)(2,1)} custom-call(s32[1,512]{1,0:T(1,128)S(1)} %copy-done.2, s32[2,4]{1,0:T(2,128)S(1)} %bitcast.10, s32[4]{0:T(128)S(1)} %copy-done.4, bf16[32,16,256]{2,1,0:T(8,128)(2,1)S(1)} %collective-permute-done.47.refs_0_, bf16[9,16,256]{2,1,0:T(8,128)(2,1)} %get-tuple-element.412.refs_1_, ...), custom_call_target="tpu_custom_call", output_to_operand_aliasing={{}: (7, {})} | custom-call | tf_op jit(solution)/shard_map/place/pallas_call | solution.py:441
  51.3 0.7 %collective-permute-done.49 = f32[2,4,1024]{2,1,0:T(4,128)S(1)} collective-permute-done((f32[2,4,1024]{2,1,0:T(4,128)S(1)}, f32[2,4,1024]{2,1,0:T(4,128)S(1)}, u32[]{:S(2)}, u32[]{:S(2)}) %collective-permute-start.49) | collective-permute-done | bytes 32800 | tf_op jit(solution)/shard_map/ppermute | solution.py:544
  52.0 0.6 %add.23 = f32[2,4,1024]{2,1,0:T(4,128)} add(f32[2,4,1024]{2,1,0:T(4,128)S(1)} %project.1, f32[2,4,1024]{2,1,0:T(4,128)S(1)} %collective-permute-done.49) | non-fusion elementwise | flops 8192 | bytes 98304 | tf_op jit(solution)/shard_map/add | solution.py:544
  52.6 0.0 collective-permute-done.48.refs_0_
  52.6 0.6 %place.3 = bf16[512,16,256]{2,1,0:T(8,128)(2,1)} custom-call(s32[1,512]{1,0:T(1,128)S(1)} %copy-done.2, s32[2,4]{1,0:T(2,128)S(1)} %bitcast.11, s32[4]{0:T(128)S(1)} %copy-done.4, bf16[7,16,256]{2,1,0:T(8,128)(2,1)S(1)} %collective-permute-done.48.refs_0_, bf16[512,16,256]{2,1,0:T(8,128)(2,1)} %place.2.refs_1_), custom_call_target="tpu_custom_call", output_to_operand_aliasing={{}: (4, {})} | custom-call | tf_op jit(solution)/shard_map/place/pallas_call | solution.py:441
  (3 shorter events, 0.0 us)
Async XLA Ops:
  0.6 1.6 %copy-start.1 = (bf16[1024,1024]{1,0:T(8,128)(2,1)S(1)}, bf16[1024,1024]{1,0:T(8,128)(2,1)}, u32[]{:S(2)}) copy-start(bf16[1024,1024]{1,0:T(8,128)(2,1)} %w_query.1) | copy-start | bytes 6291460
  0.7 22.0 %collective-permute-start.46 = (bf16[26,16,256]{2,1,0:T(8,128)(2,1)S(1)}, bf16[26,16,256]{2,1,0:T(8,128)(2,1)S(1)}, u32[]{:S(2)}, u32[]{:S(2)}) collective-permute-start(bf16[26,16,256]{2,1,0:T(8,128)(2,1)S(1)} %collect.1), channel_id=1, source_target_pairs={{16,0},{20,4},{24,8},{28,12},{17,1},{21,5},{25,9},{29,13},{18,2},{... | collective-permute-start | bytes 638984 | tf_op jit(solution)/shard_map/ppermute | solution.py:487
  4.3 18.2 %copy-start.4 = (s32[4]{0:T(128)S(1)}, s32[4]{0:T(128)}, u32[]{:S(2)}) copy-start(s32[4]{0:T(128)} %lengths.5) | copy-start | bytes 52
  4.3 20.0 %copy-start.5 = (f32[1024]{0:T(1024)S(1)}, f32[1024]{0:T(1024)}, u32[]{:S(2)}) copy-start(f32[1024]{0:T(1024)} %param.78) | copy-start | bytes 12292
  4.4 19.9 %copy-start.6 = (f32[128]{0:T(128)S(1)}, f32[128]{0:T(128)}, u32[]{:S(2)}) copy-start(f32[128]{0:T(128)} %param.80) | copy-start | bytes 1540
  4.4 19.9 %copy-start.7 = (f32[128]{0:T(128)S(1)}, f32[128]{0:T(128)}, u32[]{:S(2)}) copy-start(f32[128]{0:T(128)} %param.82) | copy-start | bytes 1540
  5.1 17.5 %collective-permute-start.1 = (bf16[28,16,256]{2,1,0:T(8,128)(2,1)S(1)}, bf16[28,16,256]{2,1,0:T(8,128)(2,1)}, u32[]{:S(2)}, u32[]{:S(2)}) collective-permute-start(bf16[28,16,256]{2,1,0:T(8,128)(2,1)S(1)} %get-tuple-element.275), channel_id=1, source_target_pairs={{20,4},{21,5},{22,6},{23,7}} | collective-permute-start | bytes 688136 | tf_op jit(solution)/shard_map/cond/branch_2_fun/ppermute | solution.py:487
  22.6 24.1 %copy-start = (bf16[1024,1024]{1,0:T(8,128)(2,1)S(1)}, bf16[1024,1024]{1,0:T(8,128)(2,1)}, u32[]{:S(2)}) copy-start(bf16[1024,1024]{1,0:T(8,128)(2,1)} %w_out.1) | copy-start | bytes 6291460
  22.6 22.8 %collective-permute-start.47 = (bf16[32,16,256]{2,1,0:T(8,128)(2,1)S(1)}, bf16[32,16,256]{2,1,0:T(8,128)(2,1)S(1)}, u32[]{:S(2)}, u32[]{:S(2)}) collective-permute-start(bf16[32,16,256]{2,1,0:T(8,128)(2,1)S(1)} %get-tuple-element.406), channel_id=1, source_target_pairs={{16,0},{20,4},{24,8},{28,12},{17,1},{21,5},{25,9},{29,13},{18,2},{... | collective-permute-start | bytes 786440 | tf_op jit(solution)/shard_map/ppermute | solution.py:487
  24.3 25.3 %copy-start.2 = (s32[1,512]{1,0:T(1,128)S(1)}, s32[1,512]{1,0:T(1,128)}, u32[]{:S(2)}) copy-start(s32[1,512]{1,0:T(1,128)} %table.3) | copy-start | bytes 6148
  24.3 25.3 %copy-start.3 = (s32[4,2]{0,1:T(2,128)S(1)}, s32[4,2]{0,1:T(2,128)}, u32[]{:S(2)}) copy-start(s32[4,2]{0,1:T(2,128)} %param.87) | copy-start | bytes 100
  31.0 14.4 %collective-permute-start.35 = (bf16[26,16,256]{2,1,0:T(8,128)(2,1)S(1)}, bf16[26,16,256]{2,1,0:T(8,128)(2,1)}, u32[]{:S(2)}, u32[]{:S(2)}) collective-permute-start(bf16[26,16,256]{2,1,0:T(8,128)(2,1)S(1)} %get-tuple-element.346), channel_id=1, source_target_pairs={{20,4},{28,12},{21,5},{29,13},{22,6},{30,14},{23,7},{31,15}} | collective-permute-start | bytes 638984 | tf_op jit(solution)/shard_map/cond/branch_10_fun/ppermute | solution.py:487
  32.4 13.0 %all-to-all-start.42 = ((f32[8,1,2176]{2,1,0:T(1,128)}), f32[8,1,2176]{2,1,0:T(1,128)}, u32[]{:S(2)}, u32[]{:S(2)}) async-start(f32[8,1,2176]{2,1,0:T(1,128)} %get-tuple-element.344), calls=%async_computation.42 | async-start | bytes 139264 | tf_op jit(solution)/shard_map/cond/branch_10_fun/all_to_all | solution.py:492
  38.2 7.2 %collective-permute-start.34 = (bf16[9,16,256]{2,1,0:T(8,128)(2,1)S(1)}, bf16[9,16,256]{2,1,0:T(8,128)(2,1)}, u32[]{:S(2)}, u32[]{:S(2)}) collective-permute-start(bf16[9,16,256]{2,1,0:T(8,128)(2,1)S(1)} %get-tuple-element.345), channel_id=1, source_target_pairs={{16,0},{20,4},{24,8},{28,12},{17,1},{21,5},{25,9},{29,13},{18,2},{... | collective-permute-start | bytes 221192 | tf_op jit(solution)/shard_map/cond/branch_10_fun/ppermute | solution.py:487
  45.4 7.2 %collective-permute-start.48 = (bf16[7,16,256]{2,1,0:T(8,128)(2,1)S(1)}, bf16[7,16,256]{2,1,0:T(8,128)(2,1)S(1)}, u32[]{:S(2)}, u32[]{:S(2)}) collective-permute-start(bf16[7,16,256]{2,1,0:T(8,128)(2,1)S(1)} %get-tuple-element.408), channel_id=1, source_target_pairs={{16,0},{20,4},{24,8},{28,12},{17,1},{21,5},{25,9},{29,13},{18,2},{... | collective-permute-start | bytes 172040 | tf_op jit(solution)/shard_map/ppermute | solution.py:487
  48.1 3.9 %collective-permute-start.49 = (f32[2,4,1024]{2,1,0:T(4,128)S(1)}, f32[2,4,1024]{2,1,0:T(4,128)S(1)}, u32[]{:S(2)}, u32[]{:S(2)}) collective-permute-start(f32[2,4,1024]{2,1,0:T(4,128)S(1)} %project.1), channel_id=1, source_target_pairs={{0,2},{2,0},{1,3},{3,1},{4,6},{6,4},{5,7},{7,5},{8,10},{10,8},{9,1... | collective-permute-start | bytes 98312 | tf_op jit(solution)/shard_map/ppermute | solution.py:544
